TPU v7x, 128 devices: a whole 4x4x4 slice. The times are simulated.
128 devices in a mesh: outer: 8 (over y, core), inner: 16 (over x, z).
Axes of the slice: x: 4, y: 4, z: 4, core: 2. Of those that a mesh axis runs over, the one named last changes fastest.
Arguments:
- currents: bfloat16 [16, 262144], P(None, ('outer', 'inner')), may hold values from -6 to 6
- near_blocks: bfloat16 [1024, 16, 256, 256], P(('outer', 'inner')), may hold values from -0.09375 to 0.09375
- near_cols: int32 [1024, 16], P(('outer', 'inner')), may hold values from 0 to 1023, as said below
- row_factors: bfloat16 [8, 32, 262144], P(None, None, ('outer', 'inner')), may hold values from -0.03125 to 0.03125
- col_factors: bfloat16 [8, 32, 262144], P(None, None, ('outer', 'inner')), may hold values from -0.375 to 0.375
- resistance: float32 [262144], P(('outer', 'inner')), may hold values from 0.2 to 2
Outputs:
- voltages: float32 [16, 262144], P(None, ('outer', 'inner'))
Inputs may be any that keep to these rules, and one draw needn't show every extreme that they name: `near_cols`: blocks are owned by devices in order, 8 to a device (outer index major). Every near column lies in the row's own group or one of the two groups next to it in circular order. Among the 128 near blocks of one device's rows, at most 3 have their column on any one device, and exactly 3 have it on the owning device itself.
All inputs are finite; a program needn't handle non-finite values.
Results may differ from a plain program's by a relative error of at most 0.0016.
Values may be sent and summed in bfloat16 or wider, within the bound.
No kernel may reach another device: no remote copies, remote signals or barrier semaphores. Data moves between devices by JAX's collectives and lax.ppermute only.
A program may use at most 128 MiB of HBM per device.

v0:
```python
import jax
import jax.numpy as jnp
from jax import lax
from jax.sharding import PartitionSpec as P


def from_behind(value, axis, steps):
    count = lax.axis_size(axis)
    pairs = [(source, (source + steps) % count) for source in range(count)]
    return lax.ppermute(value, axis, pairs)


def on_device(currents, near_blocks, near_cols, row_factors, col_factors, resistance):
    sides, filaments = currents.shape
    blocks, nearby, span_width, _ = near_blocks.shape
    outer_count = lax.axis_size("outer")
    inner_count = lax.axis_size("inner")
    my_group = lax.axis_index("outer")
    by_block = currents.reshape(sides, blocks, span_width)
    products = jnp.einsum(
        "sbp,bkpq->bksq", by_block, near_blocks, preferred_element_type=jnp.float32
    )
    flat_parts = products.reshape(blocks * nearby, sides * span_width)
    flat_cols = near_cols.reshape(-1)
    target = flat_cols // blocks
    target_group = target // inner_count
    offset = (target_group - my_group + 1) % outer_count
    window_index = (
        offset * (inner_count * blocks) + target % inner_count * blocks + flat_cols % blocks
    )
    window_total = jax.ops.segment_sum(
        flat_parts, window_index, num_segments=3 * inner_count * blocks
    )
    window_total = window_total.reshape(3, inner_count * blocks, sides * span_width)
    group_sums = lax.psum_scatter(window_total, "inner", scatter_dimension=1, tiled=True)
    from_after = from_behind(group_sums[0], "outer", -1)
    from_before = from_behind(group_sums[2], "outer", 1)
    near_sum = group_sums[1] + from_after + from_before
    near_part = (
        near_sum.reshape(blocks, sides, span_width).transpose(1, 0, 2).reshape(sides, filaments)
    )
    term_local = jnp.einsum(
        "hrn,sn->hrs", row_factors, currents, preferred_element_type=jnp.float32
    )
    group_count = row_factors.shape[0]
    summed = lax.psum(term_local, "inner").astype(jnp.bfloat16)
    arrived = lax.all_to_all(summed, "outer", split_axis=0, concat_axis=0, tiled=True)
    groups = jnp.arange(group_count, dtype=jnp.int32)
    mask_column = (groups != my_group).astype(jnp.bfloat16)
    weighted = arrived * mask_column[:, None, None]
    far_part = jnp.einsum("grn,grs->sn", col_factors, weighted, preferred_element_type=jnp.float32)
    return near_part + far_part + resistance[None, :] * currents.astype(jnp.float32)


def solution(mesh):
    return jax.shard_map(
        on_device,
        mesh=mesh,
        in_specs=(
            P(None, ("outer", "inner")),
            P(("outer", "inner"), None, None, None),
            P(("outer", "inner"), None),
            P(None, None, ("outer", "inner")),
            P(None, None, ("outer", "inner")),
            P(("outer", "inner")),
        ),
        out_specs=P(None, ("outer", "inner")),
        check_vma=False,
    )
```

profile of v0, /device:TPU:1, one launch (start us, length us, event | category | flops | bytes accessed | tf_op | source)
XLA Modules:
  0.0 127.8 jit_solution(14326868481681164917)
XLA Ops:
  6.5 0.0 copy-start
  6.5 0.0 reduce-scatter.2.cloned.1.call-start
  6.5 0.9 reshape.234
  7.4 0.9 copy.11
  8.3 8.1 %fusion.6 = f32[8,16,256,16]{2,3,1,0:T(8,128)S(1)} fusion(bf16[8,16,256,256]{3,2,1,0:T(8,128)(2,1)} %param.7, bf16[16,8,256,1]{2,1,0,3:T(8,128)(2,1)S(1)} %bitcast.46), kind=kOutput, calls=%fused_computation.12 | convolution fusion | flops 268435456 | bytes 18939904 | tf_op jit(solution)/shard_map/sbp,bkpq->bksq/dot_general | solution.py:20
  16.3 1.6 %copy.12 = f32[16,8,16,256]{3,1,2,0:T(8,128)S(1)} copy(f32[16,8,16,256]{3,2,1,0:T(8,128)S(1)} %bitcast.41) | data formatting | bytes 4194304
  18.0 0.0 copy-start.2
  18.0 6.2 %scatter_custom_fusion = f32[384,4096]{1,0:T(8,128)} fusion(s32[128]{0:T(128)S(1)} %fusion.15, f32[128,4096]{1,0:T(8,128)S(1)} %bitcast.42, f32[]{:T(128)} %constant.52.clone.1), kind=kCustom, calls=%fused_computation.1 | custom fusion | flops 524288 | bytes 6291460 | tf_op jit(solution)/shard_map/scatter-add | solution.py:31
  24.2 0.0 copy-start.1
  24.2 0.0 copy-start.3
  24.2 0.0 reduce-scatter.2.cloned.1.call-update
  24.2 0.0 copy-done.2
  24.3 1.2 copy-done.1
  25.4 0.8 fusion.4
  26.2 63.1 %psum.7 = bf16[8,32,16]{1,2,0:T(8,128)(2,1)S(1)} all-reduce(f32[8,32,16]{1,2,0:T(8,128)S(1)} %fusion.4), channel_id=1, replica_groups=mesh['outer'=8,'inner'=16] {'inner'}, use_global_device_ids=true, to_apply=%region_2.3 | all-reduce | flops 4096 | bytes 24576 | tf_op jit(solution)/shard_map/psum | solution.py:46
  89.3 0.7 reshape.253
  90.0 19.1 %all-to-all-start = ((bf16[8,2,256]{2,1,0:T(2,128)(2,1)}), bf16[8,2,256]{2,1,0:T(2,128)(2,1)S(1)}, u32[]{:S(2)}, u32[]{:S(2)}) async-start(bf16[8,2,256]{2,1,0:T(2,128)(2,1)} %reshape.253), calls=%async_computation.1 | async-start | bytes 16384 | tf_op jit(solution)/shard_map/all_to_all | solution.py:47
  109.2 4.6 %all-to-all-done = bf16[8,2,256]{2,1,0:T(2,128)(2,1)S(1)} async-done(((bf16[8,2,256]{2,1,0:T(2,128)(2,1)}), bf16[8,2,256]{2,1,0:T(2,128)(2,1)S(1)}, u32[]{:S(2)}, u32[]{:S(2)}) %all-to-all-start) | async-done | bytes 8224 | tf_op jit(solution)/shard_map/all_to_all | solution.py:47
  113.8 0.1 reshape.254
  113.9 0.0 reduce-scatter.2.cloned.1.call-done
  113.9 1.0 slice_bitcast_fusion.1
  114.9 0.7 collective-permute-start
  115.6 1.0 collective-permute-start.1
  116.6 0.0 copy-done
  116.6 0.4 convolution_bitcast_fusion
  117.0 2.2 %collective-permute-done = f32[8,4096]{1,0:T(8,128)S(1)} collective-permute-done((f32[8,4096]{1,0:T(8,128)S(1)}, f32[8,4096]{1,0:T(8,128)S(1)}, u32[]{:S(2)}, u32[]{:S(2)}) %collective-permute-start) | collective-permute-done | bytes 131104 | tf_op jit(solution)/shard_map/ppermute | solution.py:10
  119.3 0.0 collective-permute-done.1
  119.3 0.9 fusion.3
  120.3 0.0 copy-done.3
  120.3 0.7 multiply_add_fusion
  (3 shorter events, 0.1 us)
Async XLA Ops:
  6.5 110.1 %copy-start = (bf16[8,32,2048]{2,1,0:T(8,128)(2,1)S(1)}, bf16[8,32,2048]{2,1,0:T(8,128)(2,1)}, u32[]{:S(2)}) copy-start(bf16[8,32,2048]{2,1,0:T(8,128)(2,1)} %param.10) | copy-start | bytes 3145732
  6.5 107.3 %reduce-scatter.2.cloned.1.call-start = ((), (), s32[]{:S(2)}) async-start(), calls=%async_computation.2 | async-start | bytes 6684672 | tf_op jit(solution)/shard_map/reduce_scatter | solution.py:35
  18.0 6.3 %copy-start.2 = (bf16[16,2048]{1,0:T(8,128)(2,1)S(1)}, bf16[16,2048]{1,0:T(8,128)(2,1)}, u32[]{:S(2)}) copy-start(bf16[16,2048]{1,0:T(8,128)(2,1)} %param.6) | copy-start | bytes 196612
  24.2 1.2 copy-start.1
  24.2 96.0 %copy-start.3 = (f32[2048]{0:T(1024)S(1)}, f32[2048]{0:T(1024)}, u32[]{:S(2)}) copy-start(f32[2048]{0:T(1024)} %param.11) | copy-start | bytes 24580
  90.0 23.7 %all-to-all-start = ((bf16[8,2,256]{2,1,0:T(2,128)(2,1)}), bf16[8,2,256]{2,1,0:T(2,128)(2,1)S(1)}, u32[]{:S(2)}, u32[]{:S(2)}) async-start(bf16[8,2,256]{2,1,0:T(2,128)(2,1)} %reshape.253), calls=%async_computation.1 | async-start | bytes 16384 | tf_op jit(solution)/shard_map/all_to_all | solution.py:47
  114.9 4.4 %collective-permute-start = (f32[8,4096]{1,0:T(8,128)S(1)}, f32[8,4096]{1,0:T(8,128)S(1)}, u32[]{:S(2)}, u32[]{:S(2)}) collective-permute-start(f32[8,4096]{1,0:T(8,128)S(1)} %get-tuple-element.5), channel_id=1, source_target_pairs={{0,112},{16,0},{32,16},{48,32},{64,48},{80,64},{96,80},{112,96},{1... | collective-permute-start | bytes 393224 | tf_op jit(solution)/shard_map/ppermute | solution.py:10
  115.6 3.7 %collective-permute-start.1 = (f32[8,4096]{1,0:T(8,128)S(1)}, f32[8,4096]{1,0:T(8,128)S(1)}, u32[]{:S(2)}, u32[]{:S(2)}) collective-permute-start(f32[8,4096]{1,0:T(8,128)S(1)} %get-tuple-element.6), channel_id=1, source_target_pairs={{0,16},{16,32},{32,48},{48,64},{64,80},{80,96},{96,112},{112,0},{1... | collective-permute-start | bytes 393224 | tf_op jit(solution)/shard_map/ppermute | solution.py:10
Sparse Core Ops, SparseCore 0:
  24.4 83.8 reduce-scatter.1
where the time goes:
time: 129 us; the launch traced here: 128 us
  blocking collectives  63.1 us (49%)
  starting transfers between devices  20.9 us (16%)
  between operations  13.5 us (10%)
  matrix products  9.24 us (7%)
  other arithmetic  7.87 us (6%)
  waiting for transfers between devices  6.89 us (5%)
  local copies, waits for them, and re-layouts  6.37 us (5%)
    psum x1, blocking collectives, on_device(): summed = lax.psum(term_local, 'inner').astype(jnp.bfloat16)  63.1 us
    all_to_all x1, starting transfers between devices, on_device(): lax.all_to_all(summed, 'outer', split_axis=0, concat_axis=0, tiled=True)  19.1 us
    dot_general x1, matrix products, on_device(): jnp.einsum('sbp,bkpq->bksq', by_block, near_blocks, preferred_element_typ...  8.06 us
    scatter-add x1, other arithmetic, on_device(): jax.ops.segment_sum(flat_parts, window_index, num_segments=3 * inner_coun...  6.21 us
    all_to_all x1, waiting for transfers between devices, on_device(): lax.all_to_all(summed, 'outer', split_axis=0, concat_axis=0, tiled=True)  4.61 us
    unnamed x13, local copies, waits for them, and re-layouts  4.52 us
  transfers between devices with their start and end apart: 4, of which 2 were waited for; matrix products, arithmetic and copies ran while one was open for 2% of the time, Pallas kernels for 0%

commit v1 on v0

v1 whole, which is shorter than its diff:
```python
import jax
import jax.numpy as jnp
from jax import lax
from jax.experimental import pallas as pl
from jax.experimental.pallas import tpu as pltpu
from jax.sharding import PartitionSpec as P

SIDES = 16
BLK = 256
KN = 16
BPD = 8
GROUPS = 8
INNER = 16
RANK = 32
CAP = 3
SLOTS = 3 * CAP
NEAR_ROWS = SLOTS * SIDES
ROWS = NEAR_ROWS + 2 * SIDES
NOWHERE = 64.0
STEP_BLOCKS = 8
F32 = jnp.float32
BF16 = jnp.bfloat16


def lanes(shape):
    return lax.broadcasted_iota(jnp.int32, shape, len(shape) - 1)


def term_kernel(cur_ref, row_ref, out_ref):
    term = lax.dot_general(
        cur_ref[...], row_ref[...], (((1,), (1,)), ((), ())), preferred_element_type=F32
    )
    for h in range(GROUPS):
        out_ref[h] = term[:, h * RANK : (h + 1) * RANK]


def near_kernel(cols_ref, me_ref, cur_ref, blocks_ref, out_ref, meta_ref, count_ref):
    step = pl.program_id(0)
    group = me_ref[0]

    @pl.when(step == 0)
    def _():
        for t in range(3 * INNER):
            count_ref[t] = 0
        meta_ref[...] = jnp.full_like(meta_ref, NOWHERE)
        out_ref[...] = jnp.zeros_like(out_ref)

    currents = cur_ref[...]
    place = lanes((SIDES, BLK))
    for j in range(STEP_BLOCKS):
        product = jnp.dot(currents, blocks_ref[j], preferred_element_type=F32)
        col = cols_ref[step * STEP_BLOCKS + j]
        target_group = col >> 7
        target = (col >> 3) & (INNER - 1)
        apart = target_group ^ group
        kind = jnp.where(apart == 0, 0, jnp.where(apart == 1, 1, 2))
        used = count_ref[kind * INNER + target]
        count_ref[kind * INNER + target] = used + 1
        slot = kind * CAP + used
        row = pl.multiple_of(slot * SIDES, SIDES)
        out_ref[target, pl.ds(row, SIDES), :] = product.astype(BF16)
        here = place == group * RANK + slot
        meta_ref[target] = jnp.where(here, (col & (BPD - 1)).astype(F32), meta_ref[target])

    @pl.when(step == pl.num_programs(0) - 1)
    def _():
        out_ref[:, NEAR_ROWS + SIDES :, :] = meta_ref[...].astype(BF16)


def far_rows_kernel(me_ref, held_ref, arrived_ref, out_ref):
    low_half = pl.program_id(0) == 1
    whole = jnp.concatenate([arrived_ref[g] for g in range(GROUPS)], axis=1)
    high = whole.astype(BF16)

    @pl.when(jnp.logical_not(low_half))
    def _():
        out_ref[...] = jnp.broadcast_to(high[None], out_ref.shape)

    @pl.when(low_half)
    def _():
        low = whole - high.astype(F32)
        own = lanes((INNER, SIDES, BLK)) // RANK == me_ref[0]
        out_ref[...] = jnp.where(own, held_ref[...].astype(F32), low[None]).astype(BF16)


def gather_kernel(me_ref, got_ref, own_ref, core_ref, next_ref):
    lows = got_ref[:, NEAR_ROWS + SIDES :, :].reshape(INNER * SIDES, BLK)
    from_lane = lax.broadcasted_iota(jnp.int32, (BLK, BLK), 0)
    to_lane = lanes((BLK, BLK))
    spread = jnp.where(from_lane == me_ref[0] * RANK + to_lane // SIDES, float(SIDES), 0.0)
    places = jnp.dot(lows, spread.astype(BF16), preferred_element_type=F32)
    lane = lanes((SIDES, BLK))
    shift = (lane % SIDES + lane // (CAP * SIDES) * (BPD * SIDES)).astype(F32)
    rows = lax.broadcasted_iota(jnp.int32, (3 * BPD * SIDES, NEAR_ROWS), 0).astype(F32)
    total = jnp.zeros((3 * BPD * SIDES, BLK), F32)
    for i in range(INNER):
        place = (places[i * SIDES : (i + 1) * SIDES] + shift)[:, :NEAR_ROWS]
        pick = jnp.where(jnp.tile(place, (3 * BPD, 1)) == rows, 1.0, 0.0).astype(BF16)
        total += jnp.dot(pick, got_ref[i, :NEAR_ROWS, :], preferred_element_type=F32)
    size = BPD * SIDES
    own_ref[...] = total[:size]
    core_ref[...] = total[size : 2 * size]
    next_ref[...] = total[2 * size :]


def far_kernel(me_ref, got_ref, col_ref, res_ref, cur_ref, near_ref, out_ref):
    total = jnp.zeros((SIDES, BLK), F32)
    for i in range(INNER):
        high = got_ref[i, :SIDES, :].astype(F32)
        low = got_ref[i, SIDES:, :].astype(F32)
        total += high + low
    coef = jnp.where(lanes((SIDES, BLK)) // RANK == me_ref[0], 0.0, total).astype(BF16)
    far = jnp.dot(coef, col_ref[...], preferred_element_type=F32)
    far += res_ref[...] * cur_ref[...].astype(F32)
    for b in range(BPD):
        cut = slice(b * BLK, (b + 1) * BLK)
        out_ref[:, cut] = far[:, cut] + near_ref[b * SIDES : (b + 1) * SIDES, :]


def add_kernel(base_ref, core_ref, next_ref, out_ref):
    for b in range(BPD):
        cut = slice(b * BLK, (b + 1) * BLK)
        rows = slice(b * SIDES, (b + 1) * SIDES)
        out_ref[:, cut] = base_ref[:, cut] + core_ref[rows, :] + next_ref[rows, :]


def spec(*shape):
    return pl.BlockSpec(shape, lambda *_: (0,) * len(shape))


def params():
    return pltpu.CompilerParams(vmem_limit_bytes=40 * 1024 * 1024)


def cost(flops, moved):
    return pl.CostEstimate(flops=flops, bytes_accessed=moved, transcendentals=0)


def on_device(currents, near_blocks, near_cols, row_factors, col_factors, resistance):
    filaments = currents.shape[1]
    flat = GROUPS * RANK
    group = lax.axis_index("outer")
    me = jnp.stack([group, lax.axis_index("inner")]).astype(jnp.int32)
    in_smem = pl.BlockSpec(memory_space=pltpu.SMEM)

    term = pl.pallas_call(
        term_kernel,
        out_shape=jax.ShapeDtypeStruct((GROUPS, SIDES, RANK), F32),
        compiler_params=params(),
        cost_estimate=cost(2 * SIDES * flat * filaments, 1200000),
    )(currents, row_factors.reshape(flat, filaments))
    arrived = lax.all_to_all(term, "outer", split_axis=0, concat_axis=0, tiled=True)

    blocks = BPD * KN
    steps = blocks // STEP_BLOCKS
    payload_shape = jax.ShapeDtypeStruct((INNER, ROWS, BLK), BF16)
    payload = pl.pallas_call(
        near_kernel,
        out_shape=payload_shape,
        grid_spec=pltpu.PrefetchScalarGridSpec(
            num_scalar_prefetch=2,
            grid=(steps,),
            in_specs=[
                pl.BlockSpec((SIDES, BLK), lambda i, *_: (0, i * STEP_BLOCKS // KN)),
                pl.BlockSpec((STEP_BLOCKS, BLK, BLK), lambda i, *_: (i, 0, 0)),
            ],
            out_specs=spec(INNER, ROWS, BLK),
            scratch_shapes=[
                pltpu.VMEM((INNER, SIDES, BLK), F32),
                pltpu.SMEM((3 * INNER,), jnp.int32),
            ],
        ),
        compiler_params=params(),
        cost_estimate=cost(2 * blocks * SIDES * BLK * BLK, 18000000),
    )(near_cols.reshape(-1), me, currents, near_blocks.reshape(blocks, BLK, BLK))

    half = pl.BlockSpec((INNER, SIDES, BLK), lambda i, *_: (0, SLOTS + i, 0))
    payload = pl.pallas_call(
        far_rows_kernel,
        out_shape=payload_shape,
        grid=(2,),
        in_specs=[in_smem, half, spec(GROUPS, SIDES, RANK)],
        out_specs=half,
        input_output_aliases={1: 0},
        compiler_params=params(),
        cost_estimate=cost(100000, 600000),
    )(me, payload, arrived)

    got = lax.all_to_all(payload, "inner", split_axis=0, concat_axis=0, tiled=True)

    sums = jax.ShapeDtypeStruct((BPD * SIDES, BLK), F32)
    own, to_core, to_next = pl.pallas_call(
        gather_kernel,
        out_shape=(sums, sums, sums),
        in_specs=[in_smem, pl.BlockSpec(memory_space=pltpu.VMEM)],
        compiler_params=params(),
        cost_estimate=cost(2 * 384 * 144 * 16 * 256, 2000000),
    )(me, got)
    core_pairs = [(g, g ^ 1) for g in range(GROUPS)]
    next_pairs = [(g, (g + (1 if g % 2 else -1)) % GROUPS) for g in range(GROUPS)]
    from_next = lax.ppermute(to_next, "outer", next_pairs)
    from_core = lax.ppermute(to_core, "outer", core_pairs)

    base = pl.pallas_call(
        far_kernel,
        out_shape=jax.ShapeDtypeStruct((SIDES, filaments), F32),
        grid=(1,),
        in_specs=[
            in_smem,
            pl.BlockSpec((INNER, 2 * SIDES, BLK), lambda *_: (0, 0, 0)),
            spec(flat, filaments),
            spec(1, filaments),
            spec(SIDES, filaments),
            spec(BPD * SIDES, BLK),
        ],
        out_specs=spec(SIDES, filaments),
        compiler_params=params(),
        cost_estimate=cost(2 * SIDES * flat * filaments, 1600000),
    )(
        me,
        got[:, NEAR_ROWS:, :],
        col_factors.reshape(flat, filaments),
        resistance[None, :],
        currents,
        own,
    )
    return pl.pallas_call(
        add_kernel,
        out_shape=jax.ShapeDtypeStruct((SIDES, filaments), F32),
        compiler_params=params(),
        cost_estimate=cost(100000, 600000),
    )(base, from_core, from_next)


def solution(mesh):
    return jax.shard_map(
        on_device,
        mesh=mesh,
        in_specs=(
            P(None, ("outer", "inner")),
            P(("outer", "inner"), None, None, None),
            P(("outer", "inner"), None),
            P(None, None, ("outer", "inner")),
            P(None, None, ("outer", "inner")),
            P(("outer", "inner")),
        ),
        out_specs=P(None, ("outer", "inner")),
        check_vma=False,
    )
```

time: 129 us -> 63.7 us (0.49)
  blocking collectives: 63.1 us -> 27.6 us
  Pallas kernels: 0 us -> 17.9 us
  between operations: 13.5 us -> 0.08 us
  starting transfers between devices: 20.9 us -> 9.23 us
  matrix products: 9.24 us -> 0 us
  other arithmetic: 7.87 us -> 0.76 us
  waiting for transfers between devices: 6.89 us -> 2.46 us
  local copies, waits for them, and re-layouts: 6.37 us -> 5.02 us
    psum x1 -> x0, blocking collectives: 63.1 us -> none  [on_device(): summed = lax.psum(term_local, 'inner').astype(jnp.bfloat16)]
    all_to_all x0 -> x1, blocking collectives: none -> 27.6 us  [on_device(): lax.all_to_all(payload, 'inner', split_axis=0, concat_axis=0, tiled=True)]
    pallas_call x0 -> x6, Pallas kernels: none -> 17.9 us  [the longest x1 13.4 us: on_device(): pl.pallas_call(near_kernel, out_shape=payload_shape, grid_spec=pltpu.Pref...]
    all_to_all x1, starting transfers between devices: 19.1 us -> 5.97 us  [on_device(): lax.all_to_all(term, 'outer', split_axis=0, concat_axis=0, tiled=True)]
    dot_general x3 -> x0, matrix products: 9.24 us -> none  [the longest x1 8.06 us: on_device(): jnp.einsum('sbp,bkpq->bksq', by_block, near_blocks, preferred_element_typ...]
    scatter-add x1 -> x0, other arithmetic: 6.21 us -> none  [on_device(): jax.ops.segment_sum(flat_parts, window_index, num_segments=3 * inner_coun...]
    all_to_all x1, waiting for transfers between devices: 4.61 us -> 0.01 us  [on_device(): lax.all_to_all(term, 'outer', split_axis=0, concat_axis=0, tiled=True)]
    add x3 -> x0, other arithmetic: 1.65 us -> none  [the longest x1 0.93 us: on_device(): near_sum = group_sums[1] + from_after + from_before]
  transfers between devices with their start and end apart: 4 -> 3, of which waited for: 2 -> 1; matrix products, arithmetic and copies ran while one was open for 2% -> 1% of each run, Pallas kernels for 0% -> 22%
where the time goes in v1:
time: 63.7 us; the launch traced here: 63.1 us
  blocking collectives  27.6 us (43%)
  Pallas kernels  17.9 us (28%)
  starting transfers between devices  9.23 us (14%)
  local copies, waits for them, and re-layouts  5.02 us (8%)
  waiting for transfers between devices  2.46 us (4%)
  other arithmetic  0.76 us (1%)
    all_to_all x1, blocking collectives, on_device(): lax.all_to_all(payload, 'inner', split_axis=0, concat_axis=0, tiled=True)  27.6 us
    pallas_call x1, Pallas kernels, on_device(): pl.pallas_call(near_kernel, out_shape=payload_shape, grid_spec=pltpu.Pref...  13.4 us
    all_to_all x1, starting transfers between devices, on_device(): lax.all_to_all(term, 'outer', split_axis=0, concat_axis=0, tiled=True)  5.97 us
    unnamed x14, local copies, waits for them, and re-layouts  3.72 us
    ppermute x1, waiting for transfers between devices, on_device(): from_next = lax.ppermute(to_next, 'outer', next_pairs)  2.45 us
    ppermute x1, starting transfers between devices, on_device(): from_core = lax.ppermute(to_core, 'outer', core_pairs)  1.89 us
    pallas_call x1, Pallas kernels, on_device(): pl.pallas_call(gather_kernel, out_shape=(sums, sums, sums), in_specs=[in_...  1.77 us
    ppermute x1, starting transfers between devices, on_device(): from_next = lax.ppermute(to_next, 'outer', next_pairs)  1.36 us
  transfers between devices with their start and end apart: 3, of which 1 were waited for; matrix products, arithmetic and copies ran while one was open for 1% of the time, Pallas kernels for 22%

profile of v1, /device:TPU:1, one launch (start us, length us, event | category | flops | bytes accessed | tf_op | source)
XLA Modules:
  0.0 63.1 jit_solution(14155356306381653411)
XLA Ops:
  0.0 0.0 copy-start.1
  0.0 1.2 %copy-done.1 = bf16[8,32,2048]{2,1,0:T(8,128)(2,1)S(1)} copy-done((bf16[8,32,2048]{2,1,0:T(8,128)(2,1)S(1)}, bf16[8,32,2048]{2,1,0:T(8,128)(2,1)}, u32[]{:S(2)}) %copy-start.1) | copy-done | bytes 1048600
  1.2 0.0 copy-start.2
  1.2 0.8 %copy-done.2 = bf16[16,2048]{1,0:T(8,128)(2,1)S(1)} copy-done((bf16[16,2048]{1,0:T(8,128)(2,1)S(1)}, bf16[16,2048]{1,0:T(8,128)(2,1)}, u32[]{:S(2)}) %copy-start.2) | copy-done | bytes 65560
  2.1 0.4 shard_map.65
  2.5 0.7 %reshape.16 = f32[8,1,512]{2,1,0:T(1,128)} reshape(f32[8,16,32]{2,1,0:T(8,128)S(1)} %shard_map.65) | data formatting | bytes 32768
  3.2 6.0 %all-to-all-start = ((f32[8,1,512]{2,1,0:T(1,128)}), f32[8,1,512]{2,1,0:T(1,128)S(1)}, u32[]{:S(2)}, u32[]{:S(2)}) async-start(f32[8,1,512]{2,1,0:T(1,128)} %reshape.16), calls=%async_computation | async-start | bytes 32768 | tf_op jit(solution)/shard_map/all_to_all | solution.py:152
  9.2 0.8 %reshape.12.cols_ref = s32[128]{0:T(128)S(1)} reshape(s32[8,16]{1,0:T(8,128)} %param.8) | data formatting | bytes 1024 | tf_op jit(solution)/shard_map/reshape | solution.py:175
  10.0 0.1 pad_add_fusion.me_ref
  10.0 0.0 copy-start.3
  10.0 0.8 %copy-done.3 = bf16[16,2048]{1,0:T(8,128)(2,1)S(1)} copy-done((bf16[16,2048]{1,0:T(8,128)(2,1)S(1)}, bf16[16,2048]{1,0:T(8,128)(2,1)}, u32[]{:S(2)}) %copy-start.3) | copy-done | bytes 65560
  10.9 13.4 %shard_map.64.held_ref = bf16[16,176,256]{2,1,0:T(8,128)(2,1)S(1)} custom-call(s32[128]{0:T(128)S(1)} %reshape.12.cols_ref, s32[2]{0:T(128)S(1)} %pad_add_fusion.me_ref, bf16[16,2048]{1,0:T(8,128)(2,1)S(1)} %copy-done.3, bf16[128,256,256]{2,1,0:T(8,128)(2,1)} %bitcast.9), custom_call_target="tpu_custom_call" | custom-call | flops 268435456 | bytes 18000000 | tf_op jit(solution)/shard_map/pallas_call | solution.py:157
  24.3 0.0 all-to-all-done
  24.3 0.5 broadcast
  24.8 0.7 %reduce = f32[8,512]{1,0:T(8,128)S(1)} reduce(f32[8,1,512]{2,1,0:T(1,128)S(1)} %all-to-all-done, f32[]{:T(128)} %broadcast), dimensions={1}, to_apply=%all_to_all.6.reduce_sub_computation | reduce | bytes 32772 | tf_op jit(solution)/shard_map/all_to_all | solution.py:152
  25.5 0.1 reshape.17.arrived_ref
  25.6 0.8 %shard_map.66 = bf16[16,176,256]{2,1,0:T(8,128)(2,1)S(1)} custom-call(s32[2]{0:T(128)S(1)} %pad_add_fusion.me_ref, bf16[16,176,256]{2,1,0:T(8,128)(2,1)S(1)} %shard_map.64.held_ref, f32[8,16,32]{2,1,0:T(8,128)S(1)} %reshape.17.arrived_ref), custom_call_target="tpu_custom_call", output_to_operand_aliasing={{}: (1, {})} | custom-call | flops 100000 | bytes 600000 | tf_op jit(solution)/shard_map/pallas_call | solution.py:178
  26.4 27.6 %all_to_all.10.got_ref = bf16[16,176,256]{2,1,0:T(8,128)(2,1)S(1)} all-to-all(bf16[16,176,256]{2,1,0:T(8,128)(2,1)S(1)} %shard_map.66), channel_id=1, replica_groups=mesh['outer'=8,'inner'=16] {'inner'}, dimensions={0} | all-to-all | bytes 2883584 | tf_op jit(solution)/shard_map/all_to_all | solution.py:189
  54.0 0.0 copy-start
  54.0 0.0 copy-start.4
  54.0 0.0 copy-start.5
  54.0 1.8 %shard_map.67 = (f32[128,256]{1,0:T(8,128)S(1)}, f32[128,256]{1,0:T(8,128)S(1)}, f32[128,256]{1,0:T(8,128)S(1)}) custom-call(s32[2]{0:T(128)S(1)} %pad_add_fusion.me_ref, bf16[16,176,256]{2,1,0:T(8,128)(2,1)S(1)} %all_to_all.10.got_ref), custom_call_target="tpu_custom_call" | custom-call | flops 452984832 | bytes 2000000 | tf_op jit(solution)/shard_map/pallas_call | solution.py:192
  55.8 1.9 %collective-permute-start = (f32[128,256]{1,0:T(8,128)S(1)}, f32[128,256]{1,0:T(8,128)S(1)}, u32[]{:S(2)}, u32[]{:S(2)}) collective-permute-start(f32[128,256]{1,0:T(8,128)S(1)} %get-tuple-element.9), channel_id=1, source_target_pairs={{0,16},{16,0},{32,48},{48,32},{64,80},{80,64},{96,112},{112,96},{1... | collective-permute-start | bytes 393224 | tf_op jit(solution)/shard_map/ppermute | solution.py:202
  57.7 1.4 %collective-permute-start.1 = (f32[128,256]{1,0:T(8,128)S(1)}, f32[128,256]{1,0:T(8,128)S(1)}, u32[]{:S(2)}, u32[]{:S(2)}) collective-permute-start(f32[128,256]{1,0:T(8,128)S(1)} %get-tuple-element.10), channel_id=1, source_target_pairs={{0,112},{16,32},{32,16},{48,64},{64,48},{80,96},{96,80},{112,0},{1... | collective-permute-start | bytes 393224 | tf_op jit(solution)/shard_map/ppermute | solution.py:201
  59.1 0.0 copy-done
  59.1 0.0 copy-done.4
  59.1 0.0 copy-done.5
  59.1 0.8 %shard_map.68.base_ref = f32[16,2048]{1,0:T(8,128)S(1)} custom-call(s32[2]{0:T(128)S(1)} %pad_add_fusion.me_ref, bf16[16,32,256]{2,1,0:T(8,128)(2,1)S(1)} %slice.4.got_ref, bf16[256,2048]{1,0:T(8,128)(2,1)S(1)} %bitcast.6, f32[1,2048]{1,0:T(1,128)S(1)} %bitcast.8, bf16[16,2048]{1,0:T(8,128)(2,1)S(1)} %copy-done.4, f32[128,256]{1,0:T(8,128)S(1)} %get-tuple-element.8.near_ref), custom_call_target="tpu_custom_call" | custom-call | flops 16777216 | bytes 1600000 | tf_op jit(solution)/shard_map/pallas_call | solution.py:204
  59.9 0.0 collective-permute-done.core_ref
  59.9 2.5 %collective-permute-done.1.next_ref = f32[128,256]{1,0:T(8,128)S(1)} collective-permute-done((f32[128,256]{1,0:T(8,128)S(1)}, f32[128,256]{1,0:T(8,128)S(1)}, u32[]{:S(2)}, u32[]{:S(2)}) %collective-permute-start.1) | collective-permute-done | bytes 131104 | tf_op jit(solution)/shard_map/ppermute | solution.py:201
  62.4 0.7 %shard_map.69 = f32[16,2048]{1,0:T(8,128)} custom-call(f32[16,2048]{1,0:T(8,128)S(1)} %shard_map.68.base_ref, f32[128,256]{1,0:T(8,128)S(1)} %collective-permute-done.core_ref, f32[128,256]{1,0:T(8,128)S(1)} %collective-permute-done.1.next_ref), custom_call_target="tpu_custom_call" | custom-call | flops 100000 | bytes 600000 | tf_op jit(solution)/shard_map/pallas_call | solution.py:227
  (1 shorter events, 0.0 us)
Async XLA Ops:
  0.0 1.2 %copy-start.1 = (bf16[8,32,2048]{2,1,0:T(8,128)(2,1)S(1)}, bf16[8,32,2048]{2,1,0:T(8,128)(2,1)}, u32[]{:S(2)}) copy-start(bf16[8,32,2048]{2,1,0:T(8,128)(2,1)} %param.9) | copy-start | bytes 3145732
  1.2 0.8 %copy-start.2 = (bf16[16,2048]{1,0:T(8,128)(2,1)S(1)}, bf16[16,2048]{1,0:T(8,128)(2,1)}, u32[]{:S(2)}) copy-start(bf16[16,2048]{1,0:T(8,128)(2,1)} %cur_ref.5) | copy-start | bytes 196612
  3.2 21.0 %all-to-all-start = ((f32[8,1,512]{2,1,0:T(1,128)}), f32[8,1,512]{2,1,0:T(1,128)S(1)}, u32[]{:S(2)}, u32[]{:S(2)}) async-start(f32[8,1,512]{2,1,0:T(1,128)} %reshape.16), calls=%async_computation | async-start | bytes 32768 | tf_op jit(solution)/shard_map/all_to_all | solution.py:152
  10.0 0.8 %copy-start.3 = (bf16[16,2048]{1,0:T(8,128)(2,1)S(1)}, bf16[16,2048]{1,0:T(8,128)(2,1)}, u32[]{:S(2)}) copy-start(bf16[16,2048]{1,0:T(8,128)(2,1)} %cur_ref.5) | copy-start | bytes 196612
  54.0 5.1 %copy-start = (bf16[8,32,2048]{2,1,0:T(8,128)(2,1)S(1)}, bf16[8,32,2048]{2,1,0:T(8,128)(2,1)}, u32[]{:S(2)}) copy-start(bf16[8,32,2048]{2,1,0:T(8,128)(2,1)} %param.10) | copy-start | bytes 3145732
  54.0 5.1 %copy-start.4 = (bf16[16,2048]{1,0:T(8,128)(2,1)S(1)}, bf16[16,2048]{1,0:T(8,128)(2,1)}, u32[]{:S(2)}) copy-start(bf16[16,2048]{1,0:T(8,128)(2,1)} %cur_ref.5) | copy-start | bytes 196612
  54.0 5.1 %copy-start.5 = (f32[2048]{0:T(1024)S(1)}, f32[2048]{0:T(1024)}, u32[]{:S(2)}) copy-start(f32[2048]{0:T(1024)} %param.11) | copy-start | bytes 24580
  55.8 4.1 %collective-permute-start = (f32[128,256]{1,0:T(8,128)S(1)}, f32[128,256]{1,0:T(8,128)S(1)}, u32[]{:S(2)}, u32[]{:S(2)}) collective-permute-start(f32[128,256]{1,0:T(8,128)S(1)} %get-tuple-element.9), channel_id=1, source_target_pairs={{0,16},{16,0},{32,48},{48,32},{64,80},{80,64},{96,112},{112,96},{1... | collective-permute-start | bytes 393224 | tf_op jit(solution)/shard_map/ppermute | solution.py:202
  57.7 4.7 %collective-permute-start.1 = (f32[128,256]{1,0:T(8,128)S(1)}, f32[128,256]{1,0:T(8,128)S(1)}, u32[]{:S(2)}, u32[]{:S(2)}) collective-permute-start(f32[128,256]{1,0:T(8,128)S(1)} %get-tuple-element.10), channel_id=1, source_target_pairs={{0,112},{16,32},{32,16},{48,64},{64,48},{80,96},{96,80},{112,0},{1... | collective-permute-start | bytes 393224 | tf_op jit(solution)/shard_map/ppermute | solution.py:201

commit v2 on v0

v2 whole, which is shorter than its diff:
```python
import jax
import jax.numpy as jnp
from jax import lax
from jax.experimental import pallas as pl
from jax.experimental.pallas import tpu as pltpu
from jax.sharding import PartitionSpec as P

SIDES = 16
BLK = 256
KN = 16
BPD = 8
BLOCKS = BPD * KN
GROUPS = 8
INNER = 16
RANK = 32
LANES = 128
CAP = 3
KIND_ROWS = CAP * SIDES
NEAR_ROWS = 3 * KIND_ROWS
ROWS = NEAR_ROWS + 2 * SIDES
SUMS = BPD * SIDES
NOWHERE = 64
PIECE = 16
F32 = jnp.float32
BF16 = jnp.bfloat16
I32 = jnp.int32


def rows_of(shape):
    return lax.broadcasted_iota(I32, shape, 0)


def lanes_of(shape):
    return lax.broadcasted_iota(I32, shape, len(shape) - 1)


def slot_of(cols, rank, group):
    apart = (cols >> 7) ^ group
    kind = jnp.where(apart == 0, 0, jnp.where(apart == 1, 1, 2))
    return kind * CAP + rank


def send_kernel(
    cols_hbm, cur_hbm, row_hbm, blocks_hbm, out_ref,
    cols_ref, cur_ref, row_ref, blocks_ref, place_ref, dest_ref, small_sem, block_sem,
):
    cols_copy = pltpu.make_async_copy(cols_hbm, cols_ref, small_sem.at[0])
    cur_copy = pltpu.make_async_copy(cur_hbm, cur_ref, small_sem.at[1])
    row_copy = pltpu.make_async_copy(row_hbm, row_ref, small_sem.at[2])
    dest_copy = pltpu.make_async_copy(place_ref, dest_ref, small_sem.at[3])
    cols_copy.start()
    cur_copy.start()
    row_copy.start()
    block_copies = []
    for c in range(BLOCKS // PIECE):
        part = pl.ds(c * PIECE, PIECE)
        copy = pltpu.make_async_copy(blocks_hbm.at[part], blocks_ref.at[part], block_sem.at[c])
        copy.start(priority=1)
        block_copies.append(copy)
    group = lax.axis_index("outer")
    for t in range(INNER):
        out_ref[t * ROWS : t * ROWS + NEAR_ROWS, :] = jnp.zeros((NEAR_ROWS, BLK), BF16)

    cols_copy.wait()
    table = cols_ref[...].astype(F32)
    spread = jnp.concatenate(
        [jnp.broadcast_to(table[b : b + 1, :], (KN, KN)) for b in range(BPD)], axis=0
    )
    shape = (BLOCKS, KN)
    picked = jnp.where(lanes_of(shape) == rows_of(shape) % KN, spread, 0.0)
    down = jnp.sum(picked, axis=1, keepdims=True)
    square = (BLOCKS, BLOCKS)
    wide = jnp.broadcast_to(down, square)
    across = wide.T[:1, :].astype(I32)
    down = down.astype(I32)
    same = (wide.astype(I32) >> 3) == (wide.T.astype(I32) >> 3)
    above = rows_of(square) < lanes_of(square)
    below = rows_of(square) > lanes_of(square)
    rank_across = jnp.sum(jnp.where(same & above, 1.0, 0.0), axis=0, keepdims=True).astype(I32)
    rank_down = jnp.sum(jnp.where(same & below, 1.0, 0.0), axis=1, keepdims=True).astype(I32)
    target = (across >> 3) & (INNER - 1)
    first_row = target * ROWS + slot_of(across, rank_across, group) * SIDES
    place_ref[...] = jnp.broadcast_to(first_row, place_ref.shape)
    dest_copy.start()
    to_target = jnp.where(rows_of((INNER, BLOCKS)) == target, 1.0, 0.0).astype(BF16)
    lane = group * RANK + slot_of(down, rank_down, group)
    block_id = ((down & (BPD - 1)) - NOWHERE).astype(F32)
    at_slot = jnp.where(lanes_of((BLOCKS, BLK)) == lane, block_id, 0.0).astype(BF16)
    ids = jnp.dot(to_target, at_slot, preferred_element_type=F32) + float(NOWHERE)

    cur_copy.wait()
    row_copy.wait()
    term = lax.dot_general(
        cur_ref[...], row_ref[...], (((1,), (1,)), ((), ())), preferred_element_type=F32
    )
    high = term.astype(BF16)
    low = term - high.astype(F32)
    own = lanes_of((SIDES, BLK)) // RANK == group
    for t in range(INNER):
        far_row = t * ROWS + NEAR_ROWS
        out_ref[far_row : far_row + SIDES, :] = high
        out_ref[far_row + SIDES : far_row + 2 * SIDES, :] = jnp.where(
            own, ids[t : t + 1, :], low
        ).astype(BF16)

    dest_copy.wait()
    for c in range(BLOCKS // PIECE):
        block_copies[c].wait()
        for e in range(c * PIECE, (c + 1) * PIECE):
            b = e // KN
            currents = cur_ref[:, b * BLK : (b + 1) * BLK]
            product = jnp.dot(currents, blocks_ref[e], preferred_element_type=F32)
            row = pl.multiple_of(dest_ref[0, e], SIDES)
            out_ref[pl.ds(row, SIDES), :] = product.astype(BF16)


def places_of(got_ref):
    group = lax.axis_index("outer")
    lows = got_ref[:, NEAR_ROWS + SIDES :, :].reshape(INNER * SIDES, BLK)
    square = (BLK, BLK)
    expand = rows_of(square) == group * RANK + lanes_of(square) // SIDES
    expand = jnp.where(expand, float(SIDES), 0.0).astype(BF16)
    places = jnp.dot(lows, expand, preferred_element_type=F32)
    lane = lanes_of((INNER * SIDES, BLK))
    return places + (lane % SIDES + lane // KIND_ROWS * SUMS).astype(F32)


def add_slots(got_ref, places, first_kind, kinds):
    start = first_kind * KIND_ROWS
    stop = start + kinds * KIND_ROWS
    rows = (rows_of((kinds * SUMS, stop - start)) + first_kind * SUMS).astype(F32)
    total = jnp.zeros((kinds * SUMS, BLK), F32)
    for i in range(INNER):
        place = places[i * SIDES : (i + 1) * SIDES, start:stop]
        pick = jnp.where(jnp.tile(place, (kinds * BPD, 1)) == rows, 1.0, 0.0).astype(BF16)
        total += jnp.dot(pick, got_ref[i, start:stop, :], preferred_element_type=F32)
    return total


def sum_kernel(got_ref, core_ref, next_ref, coef_ref):
    total = add_slots(got_ref, places_of(got_ref), 1, 2)
    core_ref[...] = total[:SUMS]
    next_ref[...] = total[SUMS:]
    coef = jnp.zeros((SIDES, BLK), F32)
    for i in range(INNER):
        high = got_ref[i, NEAR_ROWS : NEAR_ROWS + SIDES, :].astype(F32)
        low = got_ref[i, NEAR_ROWS + SIDES :, :].astype(F32)
        coef += high + low
    coef_ref[...] = jnp.zeros_like(coef_ref)
    for h in range(GROUPS):
        coef_ref[h, :, :RANK] = coef[:, h * RANK : (h + 1) * RANK].astype(BF16)


def own_kernel(got_ref, res_ref, cur_ref, out_ref):
    total = add_slots(got_ref, places_of(got_ref), 0, 1)
    for b in range(BPD):
        cut = slice(b * BLK, (b + 1) * BLK)
        diagonal = res_ref[:, cut] * cur_ref[:, cut].astype(F32)
        out_ref[:, cut] = diagonal + total[b * SIDES : (b + 1) * SIDES, :]


def final_kernel(coef_ref, col_ref, base_ref, core_ref, next_ref, out_ref):
    coef = jnp.concatenate([coef_ref[g, :, :RANK] for g in range(GROUPS)], axis=1)
    own = lanes_of((SIDES, BLK)) // RANK == lax.axis_index("outer")
    coef = jnp.where(own, 0.0, coef.astype(F32)).astype(BF16)
    far = jnp.dot(coef, col_ref[...], preferred_element_type=F32)
    for b in range(BPD):
        cut = slice(b * BLK, (b + 1) * BLK)
        rows = slice(b * SIDES, (b + 1) * SIDES)
        near = base_ref[:, cut] + core_ref[rows, :] + next_ref[rows, :]
        out_ref[:, cut] = far[:, cut] + near


def params(mebibytes=12):
    return pltpu.CompilerParams(vmem_limit_bytes=mebibytes * 1024 * 1024)


def cost(flops, moved):
    return pl.CostEstimate(flops=flops, bytes_accessed=moved, transcendentals=0)


def on_device(currents, near_blocks, near_cols, row_factors, col_factors, resistance):
    filaments = currents.shape[1]
    flat = GROUPS * RANK
    in_vmem = pl.BlockSpec(memory_space=pltpu.VMEM)
    anywhere = pl.BlockSpec(memory_space=pl.ANY)

    payload = pl.pallas_call(
        send_kernel,
        out_shape=jax.ShapeDtypeStruct((INNER * ROWS, BLK), BF16),
        in_specs=[anywhere] * 4,
        out_specs=in_vmem,
        scratch_shapes=[
            pltpu.VMEM((BPD, KN), I32),
            pltpu.VMEM((SIDES, filaments), BF16),
            pltpu.VMEM((flat, filaments), BF16),
            pltpu.VMEM((BLOCKS, BLK, BLK), BF16),
            pltpu.VMEM((8, BLOCKS), I32),
            pltpu.SMEM((8, BLOCKS), I32),
            pltpu.SemaphoreType.DMA((4,)),
            pltpu.SemaphoreType.DMA((BLOCKS // PIECE,)),
        ],
        compiler_params=params(56),
        cost_estimate=cost(2 * BLOCKS * SIDES * BLK * BLK, 18000000),
    )(
        near_cols,
        currents,
        row_factors.reshape(flat, filaments),
        near_blocks.reshape(BLOCKS, BLK, BLK),
    )

    got = lax.all_to_all(
        payload.reshape(INNER, ROWS, BLK), "inner", split_axis=0, concat_axis=0, tiled=True
    )

    sums = jax.ShapeDtypeStruct((SUMS, BLK), F32)
    to_core, to_next, coef = pl.pallas_call(
        sum_kernel,
        out_shape=(sums, sums, jax.ShapeDtypeStruct((GROUPS, SIDES, LANES), BF16)),
        compiler_params=params(),
        cost_estimate=cost(2 * 256 * 96 * 16 * 256, 2000000),
    )(got)
    core_pairs = [(g, g ^ 1) for g in range(GROUPS)]
    next_pairs = [(g, (g + (1 if g % 2 else -1)) % GROUPS) for g in range(GROUPS)]
    from_next = lax.ppermute(to_next, "outer", next_pairs)
    from_core = lax.ppermute(to_core, "outer", core_pairs)
    coef = lax.all_to_all(coef, "outer", split_axis=0, concat_axis=0, tiled=True)

    base = pl.pallas_call(
        own_kernel,
        out_shape=jax.ShapeDtypeStruct((SIDES, filaments), F32),
        compiler_params=params(),
        cost_estimate=cost(2 * 128 * 48 * 16 * 256, 2000000),
    )(got, resistance[None, :], currents)
    return pl.pallas_call(
        final_kernel,
        out_shape=jax.ShapeDtypeStruct((SIDES, filaments), F32),
        compiler_params=params(),
        cost_estimate=cost(2 * SIDES * flat * filaments, 1600000),
    )(coef, col_factors.reshape(flat, filaments), base, from_core, from_next)


def solution(mesh):
    return jax.shard_map(
        on_device,
        mesh=mesh,
        in_specs=(
            P(None, ("outer", "inner")),
            P(("outer", "inner"), None, None, None),
            P(("outer", "inner"), None),
            P(None, None, ("outer", "inner")),
            P(None, None, ("outer", "inner")),
            P(("outer", "inner")),
        ),
        out_specs=P(None, ("outer", "inner")),
        check_vma=False,
    )
```

time: 129 us -> 52.1 us (0.40)
  blocking collectives: 63.1 us -> 28.1 us
  between operations: 13.5 us -> 0.03 us
  starting transfers between devices: 20.9 us -> 8.76 us
  Pallas kernels: 0 us -> 11 us
  matrix products: 9.24 us -> 0 us
  other arithmetic: 7.87 us -> 0 us
  local copies, waits for them, and re-layouts: 6.37 us -> 0.01 us
  waiting for transfers between devices: 6.89 us -> 4.08 us
    psum x1 -> x0, blocking collectives: 63.1 us -> none  [on_device(): summed = lax.psum(term_local, 'inner').astype(jnp.bfloat16)]
    all_to_all x0 -> x1, blocking collectives: none -> 28.1 us  [on_device(): lax.all_to_all(payload.reshape(INNER, ROWS, BLK), 'inner', split_axis=0,...]
    all_to_all x1, starting transfers between devices: 19.1 us -> 5.19 us  [on_device(): lax.all_to_all(coef, 'outer', split_axis=0, concat_axis=0, tiled=True)]
    pallas_call x0 -> x4, Pallas kernels: none -> 11 us  [the longest x1 7.81 us: on_device(): pl.pallas_call(send_kernel, out_shape=jax.ShapeDtypeStruct((INNER * ROWS,...]
    dot_general x3 -> x0, matrix products: 9.24 us -> none  [the longest x1 8.06 us: on_device(): jnp.einsum('sbp,bkpq->bksq', by_block, near_blocks, preferred_element_typ...]
    scatter-add x1 -> x0, other arithmetic: 6.21 us -> none  [on_device(): jax.ops.segment_sum(flat_parts, window_index, num_segments=3 * inner_coun...]
    unnamed x13 -> x6, local copies, waits for them, and re-layouts: 4.52 us -> 0.01 us
    ppermute x2, waiting for transfers between devices: 2.24 us -> 0.01 us  [the longest x1 0.01 us: on_device(): from_core = lax.ppermute(to_core, 'outer', core_pairs)]
  transfers between devices with their start and end apart: 4 -> 3, of which waited for: 2 -> 1; matrix products, arithmetic and copies ran while one was open for 2% -> 0% of each run, Pallas kernels for 0% -> 1%
where the time goes in v2:
time: 52.1 us; the launch traced here: 51.9 us
  blocking collectives  28.1 us (54%)
  Pallas kernels  11 us (21%)
  starting transfers between devices  8.76 us (17%)
  waiting for transfers between devices  4.08 us (8%)
    all_to_all x1, blocking collectives, on_device(): lax.all_to_all(payload.reshape(INNER, ROWS, BLK), 'inner', split_axis=0,...  28.1 us
    pallas_call x1, Pallas kernels, on_device(): pl.pallas_call(send_kernel, out_shape=jax.ShapeDtypeStruct((INNER * ROWS,...  7.81 us
    all_to_all x1, starting transfers between devices, on_device(): lax.all_to_all(coef, 'outer', split_axis=0, concat_axis=0, tiled=True)  5.19 us
    all_to_all x1, waiting for transfers between devices, on_device(): lax.all_to_all(coef, 'outer', split_axis=0, concat_axis=0, tiled=True)  4.08 us
    ppermute x1, starting transfers between devices, on_device(): from_core = lax.ppermute(to_core, 'outer', core_pairs)  2.38 us
    pallas_call x1, Pallas kernels, on_device(): pl.pallas_call(sum_kernel, out_shape=(sums, sums, jax.ShapeDtypeStruct((G...  1.56 us
    ppermute x1, starting transfers between devices, on_device(): from_next = lax.ppermute(to_next, 'outer', next_pairs)  1.19 us
  transfers between devices with their start and end apart: 3, of which 1 were waited for; matrix products, arithmetic and copies ran while one was open for 0% of the time, Pallas kernels for 1%

profile of v2, /device:TPU:1, one launch (start us, length us, event | category | flops | bytes accessed | tf_op | source)
XLA Modules:
  0.0 51.9 jit_solution(12439075231338077535)
XLA Ops:
  0.0 7.8 %shard_map.64 = bf16[2816,256]{1,0:T(8,128)(2,1)} custom-call(s32[8,16]{1,0:T(8,128)} %cols_hbm.1, bf16[16,2048]{1,0:T(8,128)(2,1)} %cur_ref.1, bf16[256,2048]{1,0:T(8,128)(2,1)} %bitcast.9, bf16[128,256,256]{2,1,0:T(8,128)(2,1)} %bitcast.7), custom_call_target="tpu_custom_call" | custom-call | flops 268435456 | bytes 18000000 | tf_op jit(solution)/shard_map/pallas_call | solution.py:188
  7.8 28.1 %all_to_all.10.got_ref = bf16[16,176,256]{2,1,0:T(8,128)(2,1)S(1)} all-to-all(bf16[16,176,256]{2,1,0:T(8,128)(2,1)} %bitcast.8), channel_id=1, replica_groups=mesh['outer'=8,'inner'=16] {'inner'}, dimensions={0} | all-to-all | bytes 2883584 | tf_op jit(solution)/shard_map/all_to_all | solution.py:212
  35.9 0.0 copy-start.1
  35.9 0.0 copy-start.2
  35.9 0.0 copy-start
  35.9 1.6 %shard_map.65 = (f32[128,256]{1,0:T(8,128)S(1)}, f32[128,256]{1,0:T(8,128)S(1)}, bf16[8,16,128]{2,1,0:T(8,128)(2,1)}) custom-call(bf16[16,176,256]{2,1,0:T(8,128)(2,1)S(1)} %all_to_all.10.got_ref), custom_call_target="tpu_custom_call" | custom-call | flops 201326592 | bytes 2000000 | tf_op jit(solution)/shard_map/pallas_call | solution.py:217
  37.4 2.4 %collective-permute-start = (f32[128,256]{1,0:T(8,128)S(1)}, f32[128,256]{1,0:T(8,128)S(1)}, u32[]{:S(2)}, u32[]{:S(2)}) collective-permute-start(f32[128,256]{1,0:T(8,128)S(1)} %get-tuple-element.9), channel_id=1, source_target_pairs={{0,16},{16,0},{32,48},{48,32},{64,80},{80,64},{96,112},{112,96},{1... | collective-permute-start | bytes 393224 | tf_op jit(solution)/shard_map/ppermute | solution.py:226
  39.8 1.2 %collective-permute-start.1 = (f32[128,256]{1,0:T(8,128)S(1)}, f32[128,256]{1,0:T(8,128)S(1)}, u32[]{:S(2)}, u32[]{:S(2)}) collective-permute-start(f32[128,256]{1,0:T(8,128)S(1)} %get-tuple-element.10), channel_id=1, source_target_pairs={{0,112},{16,32},{32,16},{48,64},{64,48},{80,96},{96,80},{112,0},{1... | collective-permute-start | bytes 393224 | tf_op jit(solution)/shard_map/ppermute | solution.py:225
  41.0 5.2 %all-to-all-start.1 = ((bf16[8,16,128]{2,1,0:T(8,128)(2,1)}), bf16[8,16,128]{2,1,0:T(8,128)(2,1)S(1)}, u32[]{:S(2)}, u32[]{:S(2)}) async-start(bf16[8,16,128]{2,1,0:T(8,128)(2,1)} %get-tuple-element.8), calls=%async_computation.1 | async-start | bytes 65536 | tf_op jit(solution)/shard_map/all_to_all | solution.py:227
  46.2 0.0 copy-done.1
  46.2 0.0 copy-done.2
  46.2 0.6 %shard_map.66.base_ref = f32[16,2048]{1,0:T(8,128)S(1)} custom-call(bf16[16,176,256]{2,1,0:T(8,128)(2,1)S(1)} %all_to_all.10.got_ref, f32[1,2048]{1,0:T(1,128)S(1)} %bitcast.6, bf16[16,2048]{1,0:T(8,128)(2,1)S(1)} %copy-done.1), custom_call_target="tpu_custom_call" | custom-call | flops 50331648 | bytes 2000000 | tf_op jit(solution)/shard_map/pallas_call | solution.py:229
  46.9 4.1 %all-to-all-done.1.coef_ref = bf16[8,16,128]{2,1,0:T(8,128)(2,1)S(1)} async-done(((bf16[8,16,128]{2,1,0:T(8,128)(2,1)}), bf16[8,16,128]{2,1,0:T(8,128)(2,1)S(1)}, u32[]{:S(2)}, u32[]{:S(2)}) %all-to-all-start.1) | async-done | bytes 32800 | tf_op jit(solution)/shard_map/all_to_all | solution.py:227
  50.9 0.0 collective-permute-done.core_ref
  50.9 0.0 collective-permute-done.1.next_ref
  50.9 0.0 copy-done
  51.0 0.9 %shard_map.67 = f32[16,2048]{1,0:T(8,128)} custom-call(bf16[8,16,128]{2,1,0:T(8,128)(2,1)S(1)} %all-to-all-done.1.coef_ref, bf16[256,2048]{1,0:T(8,128)(2,1)S(1)} %bitcast.5, f32[16,2048]{1,0:T(8,128)S(1)} %shard_map.66.base_ref, f32[128,256]{1,0:T(8,128)S(1)} %collective-permute-done.core_ref, f32[128,256]{1,0:T(8,128)S(1)} %collective-permute-done.1.next_ref), custom_call_target="tpu_custom_call" | custom-call | flops 16777216 | bytes 1600000 | tf_op jit(solution)/shard_map/pallas_call | solution.py:235
Async XLA Ops:
  35.9 10.3 %copy-start.1 = (bf16[16,2048]{1,0:T(8,128)(2,1)S(1)}, bf16[16,2048]{1,0:T(8,128)(2,1)}, u32[]{:S(2)}) copy-start(bf16[16,2048]{1,0:T(8,128)(2,1)} %cur_ref.1) | copy-start | bytes 196612
  35.9 10.3 %copy-start.2 = (f32[2048]{0:T(1024)S(1)}, f32[2048]{0:T(1024)}, u32[]{:S(2)}) copy-start(f32[2048]{0:T(1024)} %param.11) | copy-start | bytes 24580
  35.9 15.1 %copy-start = (bf16[8,32,2048]{2,1,0:T(8,128)(2,1)S(1)}, bf16[8,32,2048]{2,1,0:T(8,128)(2,1)}, u32[]{:S(2)}) copy-start(bf16[8,32,2048]{2,1,0:T(8,128)(2,1)} %param.10) | copy-start | bytes 3145732
  37.4 13.5 %collective-permute-start = (f32[128,256]{1,0:T(8,128)S(1)}, f32[128,256]{1,0:T(8,128)S(1)}, u32[]{:S(2)}, u32[]{:S(2)}) collective-permute-start(f32[128,256]{1,0:T(8,128)S(1)} %get-tuple-element.9), channel_id=1, source_target_pairs={{0,16},{16,0},{32,48},{48,32},{64,80},{80,64},{96,112},{112,96},{1... | collective-permute-start | bytes 393224 | tf_op jit(solution)/shard_map/ppermute | solution.py:226
  39.8 11.1 %collective-permute-start.1 = (f32[128,256]{1,0:T(8,128)S(1)}, f32[128,256]{1,0:T(8,128)S(1)}, u32[]{:S(2)}, u32[]{:S(2)}) collective-permute-start(f32[128,256]{1,0:T(8,128)S(1)} %get-tuple-element.10), channel_id=1, source_target_pairs={{0,112},{16,32},{32,16},{48,64},{64,48},{80,96},{96,80},{112,0},{1... | collective-permute-start | bytes 393224 | tf_op jit(solution)/shard_map/ppermute | solution.py:225
  41.0 9.9 %all-to-all-start.1 = ((bf16[8,16,128]{2,1,0:T(8,128)(2,1)}), bf16[8,16,128]{2,1,0:T(8,128)(2,1)S(1)}, u32[]{:S(2)}, u32[]{:S(2)}) async-start(bf16[8,16,128]{2,1,0:T(8,128)(2,1)} %get-tuple-element.8), calls=%async_computation.1 | async-start | bytes 65536 | tf_op jit(solution)/shard_map/all_to_all | solution.py:227

commit v3 on v2

--- a/solution.py
+++ b/solution.py
@@ -137,22 +137,24 @@
     return total
 
 
-def sum_kernel(got_ref, core_ref, next_ref, coef_ref):
-    total = add_slots(got_ref, places_of(got_ref), 1, 2)
-    core_ref[...] = total[:SUMS]
-    next_ref[...] = total[SUMS:]
+def coef_kernel(got_ref, coef_ref):
     coef = jnp.zeros((SIDES, BLK), F32)
     for i in range(INNER):
-        high = got_ref[i, NEAR_ROWS : NEAR_ROWS + SIDES, :].astype(F32)
-        low = got_ref[i, NEAR_ROWS + SIDES :, :].astype(F32)
+        high = got_ref[i, :SIDES, :].astype(F32)
+        low = got_ref[i, SIDES:, :].astype(F32)
         coef += high + low
     coef_ref[...] = jnp.zeros_like(coef_ref)
     for h in range(GROUPS):
         coef_ref[h, :, :RANK] = coef[:, h * RANK : (h + 1) * RANK].astype(BF16)
 
 
-def own_kernel(got_ref, res_ref, cur_ref, out_ref):
-    total = add_slots(got_ref, places_of(got_ref), 0, 1)
+def sum_kernel(got_ref, res_ref, cur_ref, after_ref, core_ref, next_ref, out_ref):
+    del after_ref
+    places = places_of(got_ref)
+    total = add_slots(got_ref, places, 1, 2)
+    core_ref[...] = total[:SUMS]
+    next_ref[...] = total[SUMS:]
+    total = add_slots(got_ref, places, 0, 1)
     for b in range(BPD):
         cut = slice(b * BLK, (b + 1) * BLK)
         diagonal = res_ref[:, cut] * cur_ref[:, cut].astype(F32)
@@ -177,6 +179,10 @@
 
 def cost(flops, moved):
     return pl.CostEstimate(flops=flops, bytes_accessed=moved, transcendentals=0)
+
+
+def in_hbm(array):
+    return pltpu.with_memory_space_constraint(array, pltpu.HBM)
 
 
 def on_device(currents, near_blocks, near_cols, row_factors, col_factors, resistance):
@@ -200,38 +206,39 @@
             pltpu.SemaphoreType.DMA((4,)),
             pltpu.SemaphoreType.DMA((BLOCKS // PIECE,)),
         ],
-        compiler_params=params(56),
+        compiler_params=params(50),
         cost_estimate=cost(2 * BLOCKS * SIDES * BLK * BLK, 18000000),
     )(
-        near_cols,
-        currents,
-        row_factors.reshape(flat, filaments),
-        near_blocks.reshape(BLOCKS, BLK, BLK),
+        in_hbm(near_cols),
+        in_hbm(currents),
+        in_hbm(row_factors.reshape(flat, filaments)),
+        in_hbm(near_blocks.reshape(BLOCKS, BLK, BLK)),
     )
 
     got = lax.all_to_all(
         payload.reshape(INNER, ROWS, BLK), "inner", split_axis=0, concat_axis=0, tiled=True
     )
 
+    coef = pl.pallas_call(
+        coef_kernel,
+        out_shape=jax.ShapeDtypeStruct((GROUPS, SIDES, LANES), BF16),
+        compiler_params=params(),
+        cost_estimate=cost(200000, 300000),
+    )(got[:, NEAR_ROWS:, :])
     sums = jax.ShapeDtypeStruct((SUMS, BLK), F32)
-    to_core, to_next, coef = pl.pallas_call(
+    to_core, to_next, base = pl.pallas_call(
         sum_kernel,
-        out_shape=(sums, sums, jax.ShapeDtypeStruct((GROUPS, SIDES, LANES), BF16)),
+        out_shape=(sums, sums, jax.ShapeDtypeStruct((SIDES, filaments), F32)),
+        in_specs=[in_vmem] * 3 + [anywhere],
         compiler_params=params(),
-        cost_estimate=cost(2 * 256 * 96 * 16 * 256, 2000000),
-    )(got)
+        cost_estimate=cost(2 * 384 * 96 * 16 * 256, 2000000),
+    )(got, resistance[None, :], currents, coef)
     core_pairs = [(g, g ^ 1) for g in range(GROUPS)]
     next_pairs = [(g, (g + (1 if g % 2 else -1)) % GROUPS) for g in range(GROUPS)]
     from_next = lax.ppermute(to_next, "outer", next_pairs)
     from_core = lax.ppermute(to_core, "outer", core_pairs)
     coef = lax.all_to_all(coef, "outer", split_axis=0, concat_axis=0, tiled=True)
 
-    base = pl.pallas_call(
-        own_kernel,
-        out_shape=jax.ShapeDtypeStruct((SIDES, filaments), F32),
-        compiler_params=params(),
-        cost_estimate=cost(2 * 128 * 48 * 16 * 256, 2000000),
-    )(got, resistance[None, :], currents)
     return pl.pallas_call(
         final_kernel,
         out_shape=jax.ShapeDtypeStruct((SIDES, filaments), F32),

time: 52.1 us -> 50 us (0.960)
  blocking collectives: 28.1 us -> 36.9 us
  starting transfers between devices: 8.76 us -> 3.74 us
  waiting for transfers between devices: 4.08 us -> 0.01 us
  Pallas kernels: 11 us -> 9.09 us
    all_to_all x0 -> x1, blocking collectives: none -> 8.92 us  [on_device(): lax.all_to_all(coef, 'outer', split_axis=0, concat_axis=0, tiled=True)]
    all_to_all x1 -> x0, starting transfers between devices: 5.19 us -> none  [on_device(): lax.all_to_all(coef, 'outer', split_axis=0, concat_axis=0, tiled=True)]
    all_to_all x1 -> x0, waiting for transfers between devices: 4.08 us -> none  [on_device(): lax.all_to_all(coef, 'outer', split_axis=0, concat_axis=0, tiled=True)]
    pallas_call x1, Pallas kernels: 7.81 us -> 6.77 us  [on_device(): pl.pallas_call(send_kernel, out_shape=jax.ShapeDtypeStruct((INNER * ROWS,...]
    pallas_call x2, Pallas kernels: 2.2 us -> 1.37 us  [the longest x1 1.26 us: on_device(): pl.pallas_call(sum_kernel, out_shape=(sums, sums, jax.ShapeDtypeStruct((S...]
  transfers between devices with their start and end apart: 3 -> 2, of which waited for: 1 -> 0; matrix products, arithmetic and copies ran while one was open for 0% -> 0% of each run, Pallas kernels for 1% -> 0%
where the time goes in v3:
time: 50 us; the launch traced here: 49.8 us
  blocking collectives  36.9 us (74%)
  Pallas kernels  9.09 us (18%)
  starting transfers between devices  3.74 us (7%)
    all_to_all x1, blocking collectives, on_device(): lax.all_to_all(payload.reshape(INNER, ROWS, BLK), 'inner', split_axis=0,...  28 us
    all_to_all x1, blocking collectives, on_device(): lax.all_to_all(coef, 'outer', split_axis=0, concat_axis=0, tiled=True)  8.92 us
    pallas_call x1, Pallas kernels, on_device(): pl.pallas_call(send_kernel, out_shape=jax.ShapeDtypeStruct((INNER * ROWS,...  6.77 us
    ppermute x1, starting transfers between devices, on_device(): from_core = lax.ppermute(to_core, 'outer', core_pairs)  2.47 us
    ppermute x1, starting transfers between devices, on_device(): from_next = lax.ppermute(to_next, 'outer', next_pairs)  1.27 us
    pallas_call x1, Pallas kernels, on_device(): pl.pallas_call(sum_kernel, out_shape=(sums, sums, jax.ShapeDtypeStruct((S...  1.26 us
  transfers between devices with their start and end apart: 2, of which 0 were waited for; matrix products, arithmetic and copies ran while one was open for 0% of the time, Pallas kernels for 0%

profile of v3, /device:TPU:1, one launch (start us, length us, event | category | flops | bytes accessed | tf_op | source)
XLA Modules:
  0.0 49.8 jit_solution(4317462802913984782)
XLA Ops:
  0.0 6.8 %shard_map.64 = bf16[2816,256]{1,0:T(8,128)(2,1)S(1)} custom-call(s32[8,16]{1,0:T(8,128)} %cols_hbm.1, bf16[16,2048]{1,0:T(8,128)(2,1)} %cur_ref.1, bf16[256,2048]{1,0:T(8,128)(2,1)} %bitcast.9, bf16[128,256,256]{2,1,0:T(8,128)(2,1)} %bitcast.8), custom_call_target="tpu_custom_call" | custom-call | flops 268435456 | bytes 18000000 | tf_op jit(solution)/shard_map/pallas_call | solution.py:194
  6.8 0.0 copy-start.1
  6.8 0.0 copy-start.2
  6.8 28.0 %all_to_all.10.got_ref = bf16[16,176,256]{2,1,0:T(8,128)(2,1)S(1)} all-to-all(bf16[16,176,256]{2,1,0:T(8,128)(2,1)S(1)} %bitcast.5), channel_id=1, replica_groups=mesh['outer'=8,'inner'=16] {'inner'}, dimensions={0} | all-to-all | bytes 2883584 | tf_op jit(solution)/shard_map/all_to_all | solution.py:218
  34.8 0.0 copy-start
  34.8 0.1 shard_map.65.after_ref
  34.9 0.0 copy-done.1
  34.9 0.0 copy-done.2
  34.9 1.3 %shard_map.66 = (f32[128,256]{1,0:T(8,128)S(1)}, f32[128,256]{1,0:T(8,128)S(1)}, f32[16,2048]{1,0:T(8,128)S(1)}) custom-call(bf16[16,176,256]{2,1,0:T(8,128)(2,1)S(1)} %all_to_all.10.got_ref, f32[1,2048]{1,0:T(1,128)S(1)} %bitcast.7, bf16[16,2048]{1,0:T(8,128)(2,1)S(1)} %copy-done.1, bf16[8,16,128]{2,1,0:T(8,128)(2,1)S(1)} %shard_map.65.after_ref), custom_call_target="tpu_custom_call" | custom-call | flops 301989888 | bytes 2000000 | tf_op jit(solution)/shard_map/pallas_call | solution.py:229
  36.2 2.5 %collective-permute-start = (f32[128,256]{1,0:T(8,128)S(1)}, f32[128,256]{1,0:T(8,128)S(1)}, u32[]{:S(2)}, u32[]{:S(2)}) collective-permute-start(f32[128,256]{1,0:T(8,128)S(1)} %get-tuple-element.9), channel_id=1, source_target_pairs={{0,16},{16,0},{32,48},{48,32},{64,80},{80,64},{96,112},{112,96},{1... | collective-permute-start | bytes 393224 | tf_op jit(solution)/shard_map/ppermute | solution.py:239
  38.7 1.3 %collective-permute-start.1 = (f32[128,256]{1,0:T(8,128)S(1)}, f32[128,256]{1,0:T(8,128)S(1)}, u32[]{:S(2)}, u32[]{:S(2)}) collective-permute-start(f32[128,256]{1,0:T(8,128)S(1)} %get-tuple-element.10), channel_id=1, source_target_pairs={{0,112},{16,32},{32,16},{48,64},{64,48},{80,96},{96,80},{112,0},{1... | collective-permute-start | bytes 393224 | tf_op jit(solution)/shard_map/ppermute | solution.py:238
  39.9 8.9 %all_to_all.11.coef_ref = bf16[8,16,128]{2,1,0:T(8,128)(2,1)S(1)} all-to-all(bf16[8,16,128]{2,1,0:T(8,128)(2,1)S(1)} %shard_map.65.after_ref), channel_id=1, replica_groups=mesh['outer'=8,'inner'=16] {'outer'}, dimensions={0} | all-to-all | bytes 65536 | tf_op jit(solution)/shard_map/all_to_all | solution.py:240
  48.9 0.0 collective-permute-done.core_ref
  48.9 0.0 collective-permute-done.1.next_ref
  48.9 0.0 copy-done
  48.9 0.9 %shard_map.67 = f32[16,2048]{1,0:T(8,128)} custom-call(bf16[8,16,128]{2,1,0:T(8,128)(2,1)S(1)} %all_to_all.11.coef_ref, bf16[256,2048]{1,0:T(8,128)(2,1)S(1)} %bitcast.6, f32[16,2048]{1,0:T(8,128)S(1)} %get-tuple-element.8.base_ref, f32[128,256]{1,0:T(8,128)S(1)} %collective-permute-done.core_ref, f32[128,256]{1,0:T(8,128)S(1)} %collective-permute-done.1.next_ref), custom_call_target="tpu_custom_call" | custom-call | flops 16777216 | bytes 1600000 | tf_op jit(solution)/shard_map/pallas_call | solution.py:242
  (1 shorter events, 0.0 us)
Async XLA Ops:
  6.8 28.2 %copy-start.1 = (bf16[16,2048]{1,0:T(8,128)(2,1)S(1)}, bf16[16,2048]{1,0:T(8,128)(2,1)}, u32[]{:S(2)}) copy-start(bf16[16,2048]{1,0:T(8,128)(2,1)} %cur_ref.1) | copy-start | bytes 196612
  6.8 28.1 %copy-start.2 = (f32[2048]{0:T(1024)S(1)}, f32[2048]{0:T(1024)}, u32[]{:S(2)}) copy-start(f32[2048]{0:T(1024)} %param.11) | copy-start | bytes 24580
  34.8 14.1 %copy-start = (bf16[8,32,2048]{2,1,0:T(8,128)(2,1)S(1)}, bf16[8,32,2048]{2,1,0:T(8,128)(2,1)}, u32[]{:S(2)}) copy-start(bf16[8,32,2048]{2,1,0:T(8,128)(2,1)} %param.10) | copy-start | bytes 3145732
  36.2 12.7 %collective-permute-start = (f32[128,256]{1,0:T(8,128)S(1)}, f32[128,256]{1,0:T(8,128)S(1)}, u32[]{:S(2)}, u32[]{:S(2)}) collective-permute-start(f32[128,256]{1,0:T(8,128)S(1)} %get-tuple-element.9), channel_id=1, source_target_pairs={{0,16},{16,0},{32,48},{48,32},{64,80},{80,64},{96,112},{112,96},{1... | collective-permute-start | bytes 393224 | tf_op jit(solution)/shard_map/ppermute | solution.py:239
  38.7 10.2 %collective-permute-start.1 = (f32[128,256]{1,0:T(8,128)S(1)}, f32[128,256]{1,0:T(8,128)S(1)}, u32[]{:S(2)}, u32[]{:S(2)}) collective-permute-start(f32[128,256]{1,0:T(8,128)S(1)} %get-tuple-element.10), channel_id=1, source_target_pairs={{0,112},{16,32},{32,16},{48,64},{64,48},{80,96},{96,80},{112,0},{1... | collective-permute-start | bytes 393224 | tf_op jit(solution)/shard_map/ppermute | solution.py:238

commit v4 on v3

--- a/solution.py
+++ b/solution.py
@@ -20,10 +20,19 @@
 ROWS = NEAR_ROWS + 2 * SIDES
 SUMS = BPD * SIDES
 NOWHERE = 64
+CHIPS = 4
 PIECE = 16
 F32 = jnp.float32
 BF16 = jnp.bfloat16
 I32 = jnp.int32
+
+
+def away(place):
+    return min(place, CHIPS - place)
+
+
+INNER_ORDER = sorted(range(INNER), key=lambda i: (-away(i // CHIPS) - away(i % CHIPS), i))
+OUTER_ORDER = sorted(range(GROUPS), key=lambda g: (-away(g // 2), g))
 
 
 def rows_of(shape):
@@ -78,7 +87,10 @@
     below = rows_of(square) > lanes_of(square)
     rank_across = jnp.sum(jnp.where(same & above, 1.0, 0.0), axis=0, keepdims=True).astype(I32)
     rank_down = jnp.sum(jnp.where(same & below, 1.0, 0.0), axis=1, keepdims=True).astype(I32)
-    target = (across >> 3) & (INNER - 1)
+    inner = (across >> 3) & (INNER - 1)
+    target = jnp.zeros_like(inner)
+    for position, device in enumerate(INNER_ORDER):
+        target = jnp.where(inner == device, position, target)
     first_row = target * ROWS + slot_of(across, rank_across, group) * SIDES
     place_ref[...] = jnp.broadcast_to(first_row, place_ref.shape)
     dest_copy.start()
@@ -144,8 +156,8 @@
         low = got_ref[i, SIDES:, :].astype(F32)
         coef += high + low
     coef_ref[...] = jnp.zeros_like(coef_ref)
-    for h in range(GROUPS):
-        coef_ref[h, :, :RANK] = coef[:, h * RANK : (h + 1) * RANK].astype(BF16)
+    for position, h in enumerate(OUTER_ORDER):
+        coef_ref[position, :, :RANK] = coef[:, h * RANK : (h + 1) * RANK].astype(BF16)
 
 
 def sum_kernel(got_ref, res_ref, cur_ref, after_ref, core_ref, next_ref, out_ref):
@@ -162,7 +174,8 @@
 
 
 def final_kernel(coef_ref, col_ref, base_ref, core_ref, next_ref, out_ref):
-    coef = jnp.concatenate([coef_ref[g, :, :RANK] for g in range(GROUPS)], axis=1)
+    pieces = [coef_ref[OUTER_ORDER.index(g), :, :RANK] for g in range(GROUPS)]
+    coef = jnp.concatenate(pieces, axis=1)
     own = lanes_of((SIDES, BLK)) // RANK == lax.axis_index("outer")
     coef = jnp.where(own, 0.0, coef.astype(F32)).astype(BF16)
     far = jnp.dot(coef, col_ref[...], preferred_element_type=F32)
@@ -179,6 +192,12 @@
 
 def cost(flops, moved):
     return pl.CostEstimate(flops=flops, bytes_accessed=moved, transcendentals=0)
+
+
+def exchange(array, axis, order):
+    return lax.all_to_all(
+        array, axis, split_axis=0, concat_axis=0, axis_index_groups=[order], tiled=True
+    )
 
 
 def in_hbm(array):
@@ -215,9 +234,7 @@
         in_hbm(near_blocks.reshape(BLOCKS, BLK, BLK)),
     )
 
-    got = lax.all_to_all(
-        payload.reshape(INNER, ROWS, BLK), "inner", split_axis=0, concat_axis=0, tiled=True
-    )
+    got = exchange(payload.reshape(INNER, ROWS, BLK), "inner", INNER_ORDER)
 
     coef = pl.pallas_call(
         coef_kernel,
@@ -237,7 +254,7 @@
     next_pairs = [(g, (g + (1 if g % 2 else -1)) % GROUPS) for g in range(GROUPS)]
     from_next = lax.ppermute(to_next, "outer", next_pairs)
     from_core = lax.ppermute(to_core, "outer", core_pairs)
-    coef = lax.all_to_all(coef, "outer", split_axis=0, concat_axis=0, tiled=True)
+    coef = exchange(coef, "outer", OUTER_ORDER)
 
     return pl.pallas_call(
         final_kernel,

time: 50 us -> 46.5 us (0.930)
  blocking collectives: 36.9 us -> 33.9 us
  starting transfers between devices: 3.74 us -> 3.19 us
    all_to_all x2, blocking collectives: 36.9 us -> 33.9 us  [exchange(): lax.all_to_all(array, axis, split_axis=0, concat_axis=0, axis_index_group...]
    ppermute x1, starting transfers between devices: 2.47 us -> 1.92 us  [on_device(): from_core = lax.ppermute(to_core, 'outer', core_pairs)]
where the time goes in v4:
time: 46.5 us; the launch traced here: 46.3 us
  blocking collectives  33.9 us (73%)
  Pallas kernels  9.09 us (20%)
  starting transfers between devices  3.19 us (7%)
    all_to_all x2, blocking collectives, exchange(): lax.all_to_all(array, axis, split_axis=0, concat_axis=0, axis_index_group...  33.9 us
    pallas_call x1, Pallas kernels, on_device(): pl.pallas_call(send_kernel, out_shape=jax.ShapeDtypeStruct((INNER * ROWS,...  6.77 us
    ppermute x1, starting transfers between devices, on_device(): from_core = lax.ppermute(to_core, 'outer', core_pairs)  1.92 us
    ppermute x1, starting transfers between devices, on_device(): from_next = lax.ppermute(to_next, 'outer', next_pairs)  1.27 us
    pallas_call x1, Pallas kernels, on_device(): pl.pallas_call(sum_kernel, out_shape=(sums, sums, jax.ShapeDtypeStruct((S...  1.26 us
    pallas_call x1, Pallas kernels, on_device(): pl.pallas_call(final_kernel, out_shape=jax.ShapeDtypeStruct((SIDES, filam...  0.95 us
  transfers between devices with their start and end apart: 2, of which 0 were waited for; matrix products, arithmetic and copies ran while one was open for 0% of the time, Pallas kernels for 0%

profile of v4, /device:TPU:1, one launch (start us, length us, event | category | flops | bytes accessed | tf_op | source)
XLA Modules:
  0.0 46.3 jit_solution(16050802816737892359)
XLA Ops:
  0.0 6.8 %shard_map.64 = bf16[2816,256]{1,0:T(8,128)(2,1)S(1)} custom-call(s32[8,16]{1,0:T(8,128)} %cols_hbm.1, bf16[16,2048]{1,0:T(8,128)(2,1)} %cur_ref.1, bf16[256,2048]{1,0:T(8,128)(2,1)} %bitcast.9, bf16[128,256,256]{2,1,0:T(8,128)(2,1)} %bitcast.8), custom_call_target="tpu_custom_call" | custom-call | flops 268435456 | bytes 18000000 | tf_op jit(solution)/shard_map/pallas_call | solution.py:213
  6.8 0.0 copy-start.1
  6.8 0.0 copy-start.2
  6.8 25.8 %all_to_all.10.got_ref = bf16[16,176,256]{2,1,0:T(8,128)(2,1)S(1)} all-to-all(bf16[16,176,256]{2,1,0:T(8,128)(2,1)S(1)} %bitcast.5), channel_id=1, replica_groups={{10,6,9,11,14,2,5,7,8,13,15,1,3,4,12,0},{26,22,25,27,30,18,21,23,24,29,..., dimensions={0} | all-to-all | bytes 2883584 | tf_op jit(solution)/shard_map/all_to_all | solution.py:198
  32.6 0.0 copy-start
  32.7 0.1 shard_map.65.after_ref
  32.8 0.0 copy-done.1
  32.8 0.0 copy-done.2
  32.8 1.3 %shard_map.66 = (f32[128,256]{1,0:T(8,128)S(1)}, f32[128,256]{1,0:T(8,128)S(1)}, f32[16,2048]{1,0:T(8,128)S(1)}) custom-call(bf16[16,176,256]{2,1,0:T(8,128)(2,1)S(1)} %all_to_all.10.got_ref, f32[1,2048]{1,0:T(1,128)S(1)} %bitcast.7, bf16[16,2048]{1,0:T(8,128)(2,1)S(1)} %copy-done.1, bf16[8,16,128]{2,1,0:T(8,128)(2,1)S(1)} %shard_map.65.after_ref), custom_call_target="tpu_custom_call" | custom-call | flops 301989888 | bytes 2000000 | tf_op jit(solution)/shard_map/pallas_call | solution.py:246
  34.1 1.9 %collective-permute-start = (f32[128,256]{1,0:T(8,128)S(1)}, f32[128,256]{1,0:T(8,128)S(1)}, u32[]{:S(2)}, u32[]{:S(2)}) collective-permute-start(f32[128,256]{1,0:T(8,128)S(1)} %get-tuple-element.9), channel_id=1, source_target_pairs={{0,16},{16,0},{32,48},{48,32},{64,80},{80,64},{96,112},{112,96},{1... | collective-permute-start | bytes 393224 | tf_op jit(solution)/shard_map/ppermute | solution.py:256
  36.0 1.3 %collective-permute-start.1 = (f32[128,256]{1,0:T(8,128)S(1)}, f32[128,256]{1,0:T(8,128)S(1)}, u32[]{:S(2)}, u32[]{:S(2)}) collective-permute-start(f32[128,256]{1,0:T(8,128)S(1)} %get-tuple-element.10), channel_id=1, source_target_pairs={{0,112},{16,32},{32,16},{48,64},{64,48},{80,96},{96,80},{112,0},{1... | collective-permute-start | bytes 393224 | tf_op jit(solution)/shard_map/ppermute | solution.py:255
  37.2 8.1 %all_to_all.11.coef_ref = bf16[8,16,128]{2,1,0:T(8,128)(2,1)S(1)} all-to-all(bf16[8,16,128]{2,1,0:T(8,128)(2,1)S(1)} %shard_map.65.after_ref), channel_id=1, replica_groups={{64,80,32,48,96,112,0,16},{65,81,33,49,97,113,1,17},{66,82,34,50,98,114..., dimensions={0} | all-to-all | bytes 65536 | tf_op jit(solution)/shard_map/all_to_all | solution.py:198
  45.4 0.0 collective-permute-done.core_ref
  45.4 0.0 collective-permute-done.1.next_ref
  45.4 0.0 copy-done
  45.4 0.9 %shard_map.67 = f32[16,2048]{1,0:T(8,128)} custom-call(bf16[8,16,128]{2,1,0:T(8,128)(2,1)S(1)} %all_to_all.11.coef_ref, bf16[256,2048]{1,0:T(8,128)(2,1)S(1)} %bitcast.6, f32[16,2048]{1,0:T(8,128)S(1)} %get-tuple-element.8.base_ref, f32[128,256]{1,0:T(8,128)S(1)} %collective-permute-done.core_ref, f32[128,256]{1,0:T(8,128)S(1)} %collective-permute-done.1.next_ref), custom_call_target="tpu_custom_call" | custom-call | flops 16777216 | bytes 1600000 | tf_op jit(solution)/shard_map/pallas_call | solution.py:259
  (1 shorter events, 0.0 us)
Async XLA Ops:
  6.8 26.0 %copy-start.1 = (bf16[16,2048]{1,0:T(8,128)(2,1)S(1)}, bf16[16,2048]{1,0:T(8,128)(2,1)}, u32[]{:S(2)}) copy-start(bf16[16,2048]{1,0:T(8,128)(2,1)} %cur_ref.1) | copy-start | bytes 196612
  6.8 26.0 %copy-start.2 = (f32[2048]{0:T(1024)S(1)}, f32[2048]{0:T(1024)}, u32[]{:S(2)}) copy-start(f32[2048]{0:T(1024)} %param.11) | copy-start | bytes 24580
  32.6 12.7 %copy-start = (bf16[8,32,2048]{2,1,0:T(8,128)(2,1)S(1)}, bf16[8,32,2048]{2,1,0:T(8,128)(2,1)}, u32[]{:S(2)}) copy-start(bf16[8,32,2048]{2,1,0:T(8,128)(2,1)} %param.10) | copy-start | bytes 3145732
  34.1 11.3 %collective-permute-start = (f32[128,256]{1,0:T(8,128)S(1)}, f32[128,256]{1,0:T(8,128)S(1)}, u32[]{:S(2)}, u32[]{:S(2)}) collective-permute-start(f32[128,256]{1,0:T(8,128)S(1)} %get-tuple-element.9), channel_id=1, source_target_pairs={{0,16},{16,0},{32,48},{48,32},{64,80},{80,64},{96,112},{112,96},{1... | collective-permute-start | bytes 393224 | tf_op jit(solution)/shard_map/ppermute | solution.py:256
  36.0 9.4 %collective-permute-start.1 = (f32[128,256]{1,0:T(8,128)S(1)}, f32[128,256]{1,0:T(8,128)S(1)}, u32[]{:S(2)}, u32[]{:S(2)}) collective-permute-start(f32[128,256]{1,0:T(8,128)S(1)} %get-tuple-element.10), channel_id=1, source_target_pairs={{0,112},{16,32},{32,16},{48,64},{64,48},{80,96},{96,80},{112,0},{1... | collective-permute-start | bytes 393224 | tf_op jit(solution)/shard_map/ppermute | solution.py:255

commit v5 on v4

--- a/solution.py
+++ b/solution.py
@@ -21,7 +21,7 @@
 SUMS = BPD * SIDES
 NOWHERE = 64
 CHIPS = 4
-PIECE = 16
+PIECE = 8
 F32 = jnp.float32
 BF16 = jnp.bfloat16
 I32 = jnp.int32
@@ -32,7 +32,7 @@
 
 
 INNER_ORDER = sorted(range(INNER), key=lambda i: (-away(i // CHIPS) - away(i % CHIPS), i))
-OUTER_ORDER = sorted(range(GROUPS), key=lambda g: (-away(g // 2), g))
+OUTER_ORDER = sorted(range(GROUPS), key=lambda g: (g % 2 == 0, -away(g // 2), -g))
 
 
 def rows_of(shape):
@@ -126,26 +126,27 @@
             out_ref[pl.ds(row, SIDES), :] = product.astype(BF16)
 
 
-def places_of(got_ref):
-    group = lax.axis_index("outer")
+def add_slots(got_ref, first_kind, kinds):
+    start = first_kind * KIND_ROWS
+    first_lane = lax.axis_index("outer") * RANK + first_kind * CAP
     lows = got_ref[:, NEAR_ROWS + SIDES :, :].reshape(INNER * SIDES, BLK)
-    square = (BLK, BLK)
-    expand = rows_of(square) == group * RANK + lanes_of(square) // SIDES
+    shape = (BLK, LANES)
+    expand = rows_of(shape) == first_lane + lanes_of(shape) // SIDES
     expand = jnp.where(expand, float(SIDES), 0.0).astype(BF16)
-    places = jnp.dot(lows, expand, preferred_element_type=F32)
-    lane = lanes_of((INNER * SIDES, BLK))
-    return places + (lane % SIDES + lane // KIND_ROWS * SUMS).astype(F32)
-
-
-def add_slots(got_ref, places, first_kind, kinds):
-    start = first_kind * KIND_ROWS
-    stop = start + kinds * KIND_ROWS
-    rows = (rows_of((kinds * SUMS, stop - start)) + first_kind * SUMS).astype(F32)
+    lane = lanes_of((INNER * SIDES, LANES))
+    shift = lane % SIDES + lane // KIND_ROWS * SUMS
+    shift = jnp.where(lane < kinds * KIND_ROWS, shift, 3 * SUMS).astype(F32)
+    places = jnp.dot(lows, expand, preferred_element_type=F32) + shift
+    rows = rows_of((kinds * SUMS, LANES)).astype(F32)
     total = jnp.zeros((kinds * SUMS, BLK), F32)
-    for i in range(INNER):
-        place = places[i * SIDES : (i + 1) * SIDES, start:stop]
-        pick = jnp.where(jnp.tile(place, (kinds * BPD, 1)) == rows, 1.0, 0.0).astype(BF16)
-        total += jnp.dot(pick, got_ref[i, start:stop, :], preferred_element_type=F32)
+    for i in range(0, INNER, 2):
+        picks, slots = [], []
+        for j in (i, i + 1):
+            place = jnp.tile(places[j * SIDES : (j + 1) * SIDES], (kinds * BPD, 1))
+            picks.append(jnp.where(place == rows, 1.0, 0.0).astype(BF16))
+            slots.append(got_ref[j, start : start + LANES, :])
+        pick, slot = jnp.concatenate(picks, axis=1), jnp.concatenate(slots, axis=0)
+        total += jnp.dot(pick, slot, preferred_element_type=F32)
     return total
 
 
@@ -162,11 +163,10 @@
 
 def sum_kernel(got_ref, res_ref, cur_ref, after_ref, core_ref, next_ref, out_ref):
     del after_ref
-    places = places_of(got_ref)
-    total = add_slots(got_ref, places, 1, 2)
+    total = add_slots(got_ref, 1, 2)
     core_ref[...] = total[:SUMS]
     next_ref[...] = total[SUMS:]
-    total = add_slots(got_ref, places, 0, 1)
+    total = add_slots(got_ref, 0, 1)
     for b in range(BPD):
         cut = slice(b * BLK, (b + 1) * BLK)
         diagonal = res_ref[:, cut] * cur_ref[:, cut].astype(F32)

time: 46.5 us -> 45.9 us (0.987)
  Pallas kernels: 9.09 us -> 8.55 us
where the time goes in v5:
time: 45.9 us; the launch traced here: 45.6 us
  blocking collectives  33.8 us (74%)
  Pallas kernels  8.55 us (19%)
  starting transfers between devices  3.19 us (7%)
    all_to_all x2, blocking collectives, exchange(): lax.all_to_all(array, axis, split_axis=0, concat_axis=0, axis_index_group...  33.8 us
    pallas_call x1, Pallas kernels, on_device(): pl.pallas_call(send_kernel, out_shape=jax.ShapeDtypeStruct((INNER * ROWS,...  6.68 us
    ppermute x1, starting transfers between devices, on_device(): from_core = lax.ppermute(to_core, 'outer', core_pairs)  1.92 us
    ppermute x1, starting transfers between devices, on_device(): from_next = lax.ppermute(to_next, 'outer', next_pairs)  1.27 us
    pallas_call x1, Pallas kernels, on_device(): pl.pallas_call(final_kernel, out_shape=jax.ShapeDtypeStruct((SIDES, filam...  0.95 us
  transfers between devices with their start and end apart: 2, of which 0 were waited for; matrix products, arithmetic and copies ran while one was open for 0% of the time, Pallas kernels for 0%

profile of v5, /device:TPU:1, one launch (start us, length us, event | category | flops | bytes accessed | tf_op | source)
XLA Modules:
  0.0 45.6 jit_solution(12875643905221797709)
XLA Ops:
  0.0 6.7 %shard_map.64 = bf16[2816,256]{1,0:T(8,128)(2,1)S(1)} custom-call(s32[8,16]{1,0:T(8,128)} %cols_hbm.1, bf16[16,2048]{1,0:T(8,128)(2,1)} %cur_ref.1, bf16[256,2048]{1,0:T(8,128)(2,1)} %bitcast.9, bf16[128,256,256]{2,1,0:T(8,128)(2,1)} %bitcast.8), custom_call_target="tpu_custom_call" | custom-call | flops 268435456 | bytes 18000000 | tf_op jit(solution)/shard_map/pallas_call | solution.py:213
  6.7 0.0 copy-start.1
  6.7 0.0 copy-start.2
  6.7 25.8 %all_to_all.10.got_ref = bf16[16,176,256]{2,1,0:T(8,128)(2,1)S(1)} all-to-all(bf16[16,176,256]{2,1,0:T(8,128)(2,1)S(1)} %bitcast.5), channel_id=1, replica_groups={{10,6,9,11,14,2,5,7,8,13,15,1,3,4,12,0},{26,22,25,27,30,18,21,23,24,29,..., dimensions={0} | all-to-all | bytes 2883584 | tf_op jit(solution)/shard_map/all_to_all | solution.py:198
  32.5 0.0 copy-start
  32.6 0.1 shard_map.65.after_ref
  32.7 0.0 copy-done.1
  32.7 0.0 copy-done.2
  32.7 0.8 %shard_map.66 = (f32[128,256]{1,0:T(8,128)S(1)}, f32[128,256]{1,0:T(8,128)S(1)}, f32[16,2048]{1,0:T(8,128)S(1)}) custom-call(bf16[16,176,256]{2,1,0:T(8,128)(2,1)S(1)} %all_to_all.10.got_ref, f32[1,2048]{1,0:T(1,128)S(1)} %bitcast.7, bf16[16,2048]{1,0:T(8,128)(2,1)S(1)} %copy-done.1, bf16[8,16,128]{2,1,0:T(8,128)(2,1)S(1)} %shard_map.65.after_ref), custom_call_target="tpu_custom_call" | custom-call | flops 301989888 | bytes 2000000 | tf_op jit(solution)/shard_map/pallas_call | solution.py:246
  33.5 1.9 %collective-permute-start = (f32[128,256]{1,0:T(8,128)S(1)}, f32[128,256]{1,0:T(8,128)S(1)}, u32[]{:S(2)}, u32[]{:S(2)}) collective-permute-start(f32[128,256]{1,0:T(8,128)S(1)} %get-tuple-element.9), channel_id=1, source_target_pairs={{0,16},{16,0},{32,48},{48,32},{64,80},{80,64},{96,112},{112,96},{1... | collective-permute-start | bytes 393224 | tf_op jit(solution)/shard_map/ppermute | solution.py:256
  35.4 1.3 %collective-permute-start.1 = (f32[128,256]{1,0:T(8,128)S(1)}, f32[128,256]{1,0:T(8,128)S(1)}, u32[]{:S(2)}, u32[]{:S(2)}) collective-permute-start(f32[128,256]{1,0:T(8,128)S(1)} %get-tuple-element.10), channel_id=1, source_target_pairs={{0,112},{16,32},{32,16},{48,64},{64,48},{80,96},{96,80},{112,0},{1... | collective-permute-start | bytes 393224 | tf_op jit(solution)/shard_map/ppermute | solution.py:255
  36.7 8.0 %all_to_all.11.coef_ref = bf16[8,16,128]{2,1,0:T(8,128)(2,1)S(1)} all-to-all(bf16[8,16,128]{2,1,0:T(8,128)(2,1)S(1)} %shard_map.65.after_ref), channel_id=1, replica_groups={{80,112,48,16,64,96,32,0},{81,113,49,17,65,97,33,1},{82,114,50,18,66,98..., dimensions={0} | all-to-all | bytes 65536 | tf_op jit(solution)/shard_map/all_to_all | solution.py:198
  44.7 0.0 collective-permute-done.core_ref
  44.7 0.0 collective-permute-done.1.next_ref
  44.7 0.0 copy-done
  44.7 0.9 %shard_map.67 = f32[16,2048]{1,0:T(8,128)} custom-call(bf16[8,16,128]{2,1,0:T(8,128)(2,1)S(1)} %all_to_all.11.coef_ref, bf16[256,2048]{1,0:T(8,128)(2,1)S(1)} %bitcast.6, f32[16,2048]{1,0:T(8,128)S(1)} %get-tuple-element.8.base_ref, f32[128,256]{1,0:T(8,128)S(1)} %collective-permute-done.core_ref, f32[128,256]{1,0:T(8,128)S(1)} %collective-permute-done.1.next_ref), custom_call_target="tpu_custom_call" | custom-call | flops 16777216 | bytes 1600000 | tf_op jit(solution)/shard_map/pallas_call | solution.py:259
  (1 shorter events, 0.0 us)
Async XLA Ops:
  6.7 26.0 %copy-start.1 = (bf16[16,2048]{1,0:T(8,128)(2,1)S(1)}, bf16[16,2048]{1,0:T(8,128)(2,1)}, u32[]{:S(2)}) copy-start(bf16[16,2048]{1,0:T(8,128)(2,1)} %cur_ref.1) | copy-start | bytes 196612
  6.7 26.0 %copy-start.2 = (f32[2048]{0:T(1024)S(1)}, f32[2048]{0:T(1024)}, u32[]{:S(2)}) copy-start(f32[2048]{0:T(1024)} %param.11) | copy-start | bytes 24580
  32.5 12.2 %copy-start = (bf16[8,32,2048]{2,1,0:T(8,128)(2,1)S(1)}, bf16[8,32,2048]{2,1,0:T(8,128)(2,1)}, u32[]{:S(2)}) copy-start(bf16[8,32,2048]{2,1,0:T(8,128)(2,1)} %param.10) | copy-start | bytes 3145732
  33.5 11.2 %collective-permute-start = (f32[128,256]{1,0:T(8,128)S(1)}, f32[128,256]{1,0:T(8,128)S(1)}, u32[]{:S(2)}, u32[]{:S(2)}) collective-permute-start(f32[128,256]{1,0:T(8,128)S(1)} %get-tuple-element.9), channel_id=1, source_target_pairs={{0,16},{16,0},{32,48},{48,32},{64,80},{80,64},{96,112},{112,96},{1... | collective-permute-start | bytes 393224 | tf_op jit(solution)/shard_map/ppermute | solution.py:256
  35.4 9.3 %collective-permute-start.1 = (f32[128,256]{1,0:T(8,128)S(1)}, f32[128,256]{1,0:T(8,128)S(1)}, u32[]{:S(2)}, u32[]{:S(2)}) collective-permute-start(f32[128,256]{1,0:T(8,128)S(1)} %get-tuple-element.10), channel_id=1, source_target_pairs={{0,112},{16,32},{32,16},{48,64},{64,48},{80,96},{96,80},{112,0},{1... | collective-permute-start | bytes 393224 | tf_op jit(solution)/shard_map/ppermute | solution.py:255

commit v6 on v5

--- a/solution.py
+++ b/solution.py
@@ -161,8 +161,7 @@
         coef_ref[position, :, :RANK] = coef[:, h * RANK : (h + 1) * RANK].astype(BF16)
 
 
-def sum_kernel(got_ref, res_ref, cur_ref, after_ref, core_ref, next_ref, out_ref):
-    del after_ref
+def sum_kernel(got_ref, res_ref, cur_ref, core_ref, next_ref, out_ref):
     total = add_slots(got_ref, 1, 2)
     core_ref[...] = total[:SUMS]
     next_ref[...] = total[SUMS:]
@@ -246,10 +245,10 @@
     to_core, to_next, base = pl.pallas_call(
         sum_kernel,
         out_shape=(sums, sums, jax.ShapeDtypeStruct((SIDES, filaments), F32)),
-        in_specs=[in_vmem] * 3 + [anywhere],
+        in_specs=[in_vmem] * 3,
         compiler_params=params(),
         cost_estimate=cost(2 * 384 * 96 * 16 * 256, 2000000),
-    )(got, resistance[None, :], currents, coef)
+    )(got, resistance[None, :], currents)
     core_pairs = [(g, g ^ 1) for g in range(GROUPS)]
     next_pairs = [(g, (g + (1 if g % 2 else -1)) % GROUPS) for g in range(GROUPS)]
     from_next = lax.ppermute(to_next, "outer", next_pairs)

time: 45.9 us -> 45.8 us (level)
  no operation moved by 1% of the time
where the time goes in v6:
time: 45.8 us; the launch traced here: 45.6 us
  blocking collectives  33.8 us (74%)
  Pallas kernels  8.53 us (19%)
  starting transfers between devices  3.19 us (7%)
    all_to_all x2, blocking collectives, exchange(): lax.all_to_all(array, axis, split_axis=0, concat_axis=0, axis_index_group...  33.8 us
    pallas_call x1, Pallas kernels, on_device(): pl.pallas_call(send_kernel, out_shape=jax.ShapeDtypeStruct((INNER * ROWS,...  6.68 us
    ppermute x1, starting transfers between devices, on_device(): from_core = lax.ppermute(to_core, 'outer', core_pairs)  1.92 us
    ppermute x1, starting transfers between devices, on_device(): from_next = lax.ppermute(to_next, 'outer', next_pairs)  1.27 us
    pallas_call x1, Pallas kernels, on_device(): pl.pallas_call(final_kernel, out_shape=jax.ShapeDtypeStruct((SIDES, filam...  0.95 us
  transfers between devices with their start and end apart: 2, of which 0 were waited for; matrix products, arithmetic and copies ran while one was open for 0% of the time, Pallas kernels for 0%

profile of v6, /device:TPU:1, one launch (start us, length us, event | category | flops | bytes accessed | tf_op | source)
XLA Modules:
  0.0 45.6 jit_solution(13358768910844545476)
XLA Ops:
  0.0 6.7 %shard_map.64 = bf16[2816,256]{1,0:T(8,128)(2,1)S(1)} custom-call(s32[8,16]{1,0:T(8,128)} %cols_hbm.1, bf16[16,2048]{1,0:T(8,128)(2,1)} %cur_ref.1, bf16[256,2048]{1,0:T(8,128)(2,1)} %bitcast.9, bf16[128,256,256]{2,1,0:T(8,128)(2,1)} %bitcast.8), custom_call_target="tpu_custom_call" | custom-call | flops 268435456 | bytes 18000000 | tf_op jit(solution)/shard_map/pallas_call | solution.py:212
  6.7 0.0 copy-start.1
  6.7 0.0 copy-start.2
  6.7 25.8 %all_to_all.10.got_ref = bf16[16,176,256]{2,1,0:T(8,128)(2,1)S(1)} all-to-all(bf16[16,176,256]{2,1,0:T(8,128)(2,1)S(1)} %bitcast.5), channel_id=1, replica_groups={{10,6,9,11,14,2,5,7,8,13,15,1,3,4,12,0},{26,22,25,27,30,18,21,23,24,29,..., dimensions={0} | all-to-all | bytes 2883584 | tf_op jit(solution)/shard_map/all_to_all | solution.py:197
  32.5 0.0 copy-start
  32.5 0.0 copy-done.1
  32.5 0.0 copy-done.2
  32.5 0.8 %shard_map.66 = (f32[128,256]{1,0:T(8,128)S(1)}, f32[128,256]{1,0:T(8,128)S(1)}, f32[16,2048]{1,0:T(8,128)S(1)}) custom-call(bf16[16,176,256]{2,1,0:T(8,128)(2,1)S(1)} %all_to_all.10.got_ref, f32[1,2048]{1,0:T(1,128)S(1)} %bitcast.7, bf16[16,2048]{1,0:T(8,128)(2,1)S(1)} %copy-done.1), custom_call_target="tpu_custom_call" | custom-call | flops 301989888 | bytes 2000000 | tf_op jit(solution)/shard_map/pallas_call | solution.py:245
  33.3 1.9 %collective-permute-start = (f32[128,256]{1,0:T(8,128)S(1)}, f32[128,256]{1,0:T(8,128)S(1)}, u32[]{:S(2)}, u32[]{:S(2)}) collective-permute-start(f32[128,256]{1,0:T(8,128)S(1)} %get-tuple-element.9), channel_id=1, source_target_pairs={{0,16},{16,0},{32,48},{48,32},{64,80},{80,64},{96,112},{112,96},{1... | collective-permute-start | bytes 393224 | tf_op jit(solution)/shard_map/ppermute | solution.py:255
  35.2 1.3 %collective-permute-start.1 = (f32[128,256]{1,0:T(8,128)S(1)}, f32[128,256]{1,0:T(8,128)S(1)}, u32[]{:S(2)}, u32[]{:S(2)}) collective-permute-start(f32[128,256]{1,0:T(8,128)S(1)} %get-tuple-element.10), channel_id=1, source_target_pairs={{0,112},{16,32},{32,16},{48,64},{64,48},{80,96},{96,80},{112,0},{1... | collective-permute-start | bytes 393224 | tf_op jit(solution)/shard_map/ppermute | solution.py:254
  36.5 0.1 shard_map.65
  36.7 8.0 %all_to_all.11.coef_ref = bf16[8,16,128]{2,1,0:T(8,128)(2,1)S(1)} all-to-all(bf16[8,16,128]{2,1,0:T(8,128)(2,1)S(1)} %shard_map.65), channel_id=1, replica_groups={{80,112,48,16,64,96,32,0},{81,113,49,17,65,97,33,1},{82,114,50,18,66,98..., dimensions={0} | all-to-all | bytes 65536 | tf_op jit(solution)/shard_map/all_to_all | solution.py:197
  44.7 0.0 collective-permute-done.core_ref
  44.7 0.0 collective-permute-done.1.next_ref
  44.7 0.0 copy-done
  44.7 0.9 %shard_map.67 = f32[16,2048]{1,0:T(8,128)} custom-call(bf16[8,16,128]{2,1,0:T(8,128)(2,1)S(1)} %all_to_all.11.coef_ref, bf16[256,2048]{1,0:T(8,128)(2,1)S(1)} %bitcast.6, f32[16,2048]{1,0:T(8,128)S(1)} %get-tuple-element.8.base_ref, f32[128,256]{1,0:T(8,128)S(1)} %collective-permute-done.core_ref, f32[128,256]{1,0:T(8,128)S(1)} %collective-permute-done.1.next_ref), custom_call_target="tpu_custom_call" | custom-call | flops 16777216 | bytes 1600000 | tf_op jit(solution)/shard_map/pallas_call | solution.py:258
  (1 shorter events, 0.0 us)
Async XLA Ops:
  6.7 25.8 %copy-start.1 = (bf16[16,2048]{1,0:T(8,128)(2,1)S(1)}, bf16[16,2048]{1,0:T(8,128)(2,1)}, u32[]{:S(2)}) copy-start(bf16[16,2048]{1,0:T(8,128)(2,1)} %cur_ref.1) | copy-start | bytes 196612
  6.7 25.8 %copy-start.2 = (f32[2048]{0:T(1024)S(1)}, f32[2048]{0:T(1024)}, u32[]{:S(2)}) copy-start(f32[2048]{0:T(1024)} %param.11) | copy-start | bytes 24580
  32.5 12.1 %copy-start = (bf16[8,32,2048]{2,1,0:T(8,128)(2,1)S(1)}, bf16[8,32,2048]{2,1,0:T(8,128)(2,1)}, u32[]{:S(2)}) copy-start(bf16[8,32,2048]{2,1,0:T(8,128)(2,1)} %param.10) | copy-start | bytes 3145732
  33.3 11.3 %collective-permute-start = (f32[128,256]{1,0:T(8,128)S(1)}, f32[128,256]{1,0:T(8,128)S(1)}, u32[]{:S(2)}, u32[]{:S(2)}) collective-permute-start(f32[128,256]{1,0:T(8,128)S(1)} %get-tuple-element.9), channel_id=1, source_target_pairs={{0,16},{16,0},{32,48},{48,32},{64,80},{80,64},{96,112},{112,96},{1... | collective-permute-start | bytes 393224 | tf_op jit(solution)/shard_map/ppermute | solution.py:255
  35.2 9.4 %collective-permute-start.1 = (f32[128,256]{1,0:T(8,128)S(1)}, f32[128,256]{1,0:T(8,128)S(1)}, u32[]{:S(2)}, u32[]{:S(2)}) collective-permute-start(f32[128,256]{1,0:T(8,128)S(1)} %get-tuple-element.10), channel_id=1, source_target_pairs={{0,112},{16,32},{32,16},{48,64},{64,48},{80,96},{96,80},{112,0},{1... | collective-permute-start | bytes 393224 | tf_op jit(solution)/shard_map/ppermute | solution.py:254

commit v7 on v6

--- a/solution.py
+++ b/solution.py
@@ -20,19 +20,14 @@
 ROWS = NEAR_ROWS + 2 * SIDES
 SUMS = BPD * SIDES
 NOWHERE = 64
-CHIPS = 4
 PIECE = 8
 F32 = jnp.float32
 BF16 = jnp.bfloat16
 I32 = jnp.int32
 
 
-def away(place):
-    return min(place, CHIPS - place)
-
-
-INNER_ORDER = sorted(range(INNER), key=lambda i: (-away(i // CHIPS) - away(i % CHIPS), i))
-OUTER_ORDER = sorted(range(GROUPS), key=lambda g: (g % 2 == 0, -away(g // 2), -g))
+INNER_ORDER = [10, 2, 7, 6, 1, 5, 15, 11, 14, 3, 12, 0, 9, 4, 13, 8]
+OUTER_ORDER = [5, 3, 7, 1, 4, 2, 6, 0]
 
 
 def rows_of(shape):

time: 45.8 us -> 45.6 us (level)
  no operation moved by 1% of the time
where the time goes in v7:
time: 45.6 us; the launch traced here: 45.4 us
  blocking collectives  33.6 us (74%)
  Pallas kernels  8.53 us (19%)
  starting transfers between devices  3.19 us (7%)
    all_to_all x2, blocking collectives, exchange(): lax.all_to_all(array, axis, split_axis=0, concat_axis=0, axis_index_group...  33.6 us
    pallas_call x1, Pallas kernels, on_device(): pl.pallas_call(send_kernel, out_shape=jax.ShapeDtypeStruct((INNER * ROWS,...  6.68 us
    ppermute x1, starting transfers between devices, on_device(): from_core = lax.ppermute(to_core, 'outer', core_pairs)  1.92 us
    ppermute x1, starting transfers between devices, on_device(): from_next = lax.ppermute(to_next, 'outer', next_pairs)  1.27 us
    pallas_call x1, Pallas kernels, on_device(): pl.pallas_call(final_kernel, out_shape=jax.ShapeDtypeStruct((SIDES, filam...  0.95 us
  transfers between devices with their start and end apart: 2, of which 0 were waited for; matrix products, arithmetic and copies ran while one was open for 0% of the time, Pallas kernels for 0%

profile of v7, /device:TPU:1, one launch (start us, length us, event | category | flops | bytes accessed | tf_op | source)
XLA Modules:
  0.0 45.4 jit_solution(5377198161428789831)
XLA Ops:
  0.0 6.7 %shard_map.64 = bf16[2816,256]{1,0:T(8,128)(2,1)S(1)} custom-call(s32[8,16]{1,0:T(8,128)} %cols_hbm.1, bf16[16,2048]{1,0:T(8,128)(2,1)} %cur_ref.1, bf16[256,2048]{1,0:T(8,128)(2,1)} %bitcast.9, bf16[128,256,256]{2,1,0:T(8,128)(2,1)} %bitcast.8), custom_call_target="tpu_custom_call" | custom-call | flops 268435456 | bytes 18000000 | tf_op jit(solution)/shard_map/pallas_call | solution.py:207
  6.7 0.0 copy-start.1
  6.7 0.0 copy-start.2
  6.7 25.6 %all_to_all.10.got_ref = bf16[16,176,256]{2,1,0:T(8,128)(2,1)S(1)} all-to-all(bf16[16,176,256]{2,1,0:T(8,128)(2,1)S(1)} %bitcast.5), channel_id=1, replica_groups={{10,2,7,6,1,5,15,11,14,3,12,0,9,4,13,8},{26,18,23,22,17,21,31,27,30,19,..., dimensions={0} | all-to-all | bytes 2883584 | tf_op jit(solution)/shard_map/all_to_all | solution.py:192
  32.3 0.0 copy-start
  32.3 0.0 copy-done.1
  32.3 0.0 copy-done.2
  32.3 0.8 %shard_map.66 = (f32[128,256]{1,0:T(8,128)S(1)}, f32[128,256]{1,0:T(8,128)S(1)}, f32[16,2048]{1,0:T(8,128)S(1)}) custom-call(bf16[16,176,256]{2,1,0:T(8,128)(2,1)S(1)} %all_to_all.10.got_ref, f32[1,2048]{1,0:T(1,128)S(1)} %bitcast.7, bf16[16,2048]{1,0:T(8,128)(2,1)S(1)} %copy-done.1), custom_call_target="tpu_custom_call" | custom-call | flops 301989888 | bytes 2000000 | tf_op jit(solution)/shard_map/pallas_call | solution.py:240
  33.1 1.9 %collective-permute-start = (f32[128,256]{1,0:T(8,128)S(1)}, f32[128,256]{1,0:T(8,128)S(1)}, u32[]{:S(2)}, u32[]{:S(2)}) collective-permute-start(f32[128,256]{1,0:T(8,128)S(1)} %get-tuple-element.9), channel_id=1, source_target_pairs={{0,16},{16,0},{32,48},{48,32},{64,80},{80,64},{96,112},{112,96},{1... | collective-permute-start | bytes 393224 | tf_op jit(solution)/shard_map/ppermute | solution.py:250
  35.0 1.3 %collective-permute-start.1 = (f32[128,256]{1,0:T(8,128)S(1)}, f32[128,256]{1,0:T(8,128)S(1)}, u32[]{:S(2)}, u32[]{:S(2)}) collective-permute-start(f32[128,256]{1,0:T(8,128)S(1)} %get-tuple-element.10), channel_id=1, source_target_pairs={{0,112},{16,32},{32,16},{48,64},{64,48},{80,96},{96,80},{112,0},{1... | collective-permute-start | bytes 393224 | tf_op jit(solution)/shard_map/ppermute | solution.py:249
  36.3 0.1 shard_map.65
  36.4 8.0 %all_to_all.11.coef_ref = bf16[8,16,128]{2,1,0:T(8,128)(2,1)S(1)} all-to-all(bf16[8,16,128]{2,1,0:T(8,128)(2,1)S(1)} %shard_map.65), channel_id=1, replica_groups={{80,48,112,16,64,32,96,0},{81,49,113,17,65,33,97,1},{82,50,114,18,66,34..., dimensions={0} | all-to-all | bytes 65536 | tf_op jit(solution)/shard_map/all_to_all | solution.py:192
  44.4 0.0 collective-permute-done.core_ref
  44.4 0.0 collective-permute-done.1.next_ref
  44.4 0.0 copy-done
  44.4 0.9 %shard_map.67 = f32[16,2048]{1,0:T(8,128)} custom-call(bf16[8,16,128]{2,1,0:T(8,128)(2,1)S(1)} %all_to_all.11.coef_ref, bf16[256,2048]{1,0:T(8,128)(2,1)S(1)} %bitcast.6, f32[16,2048]{1,0:T(8,128)S(1)} %get-tuple-element.8.base_ref, f32[128,256]{1,0:T(8,128)S(1)} %collective-permute-done.core_ref, f32[128,256]{1,0:T(8,128)S(1)} %collective-permute-done.1.next_ref), custom_call_target="tpu_custom_call" | custom-call | flops 16777216 | bytes 1600000 | tf_op jit(solution)/shard_map/pallas_call | solution.py:253
  (1 shorter events, 0.0 us)
Async XLA Ops:
  6.7 25.6 %copy-start.1 = (bf16[16,2048]{1,0:T(8,128)(2,1)S(1)}, bf16[16,2048]{1,0:T(8,128)(2,1)}, u32[]{:S(2)}) copy-start(bf16[16,2048]{1,0:T(8,128)(2,1)} %cur_ref.1) | copy-start | bytes 196612
  6.7 25.6 %copy-start.2 = (f32[2048]{0:T(1024)S(1)}, f32[2048]{0:T(1024)}, u32[]{:S(2)}) copy-start(f32[2048]{0:T(1024)} %param.11) | copy-start | bytes 24580
  32.3 12.2 %copy-start = (bf16[8,32,2048]{2,1,0:T(8,128)(2,1)S(1)}, bf16[8,32,2048]{2,1,0:T(8,128)(2,1)}, u32[]{:S(2)}) copy-start(bf16[8,32,2048]{2,1,0:T(8,128)(2,1)} %param.10) | copy-start | bytes 3145732
  33.1 11.4 %collective-permute-start = (f32[128,256]{1,0:T(8,128)S(1)}, f32[128,256]{1,0:T(8,128)S(1)}, u32[]{:S(2)}, u32[]{:S(2)}) collective-permute-start(f32[128,256]{1,0:T(8,128)S(1)} %get-tuple-element.9), channel_id=1, source_target_pairs={{0,16},{16,0},{32,48},{48,32},{64,80},{80,64},{96,112},{112,96},{1... | collective-permute-start | bytes 393224 | tf_op jit(solution)/shard_map/ppermute | solution.py:250
  35.0 9.4 %collective-permute-start.1 = (f32[128,256]{1,0:T(8,128)S(1)}, f32[128,256]{1,0:T(8,128)S(1)}, u32[]{:S(2)}, u32[]{:S(2)}) collective-permute-start(f32[128,256]{1,0:T(8,128)S(1)} %get-tuple-element.10), channel_id=1, source_target_pairs={{0,112},{16,32},{32,16},{48,64},{64,48},{80,96},{96,80},{112,0},{1... | collective-permute-start | bytes 393224 | tf_op jit(solution)/shard_map/ppermute | solution.py:249
